TPU v7x, 1024 devices: a whole 4x4x32 slice. The times are simulated.
1024 devices in a mesh: rep: 8 (over z_lo), table: 32 (over z_hi, y, core), tensor: 4 (over x).
Axes of the slice: x: 4, y: 4, z: 32 (z_hi: 4, z_lo: 8; z = z_hi * 8 + z_lo), core: 2. Of those that a mesh axis runs over, the one named last changes fastest.
Arguments:
- pooled: bfloat16 [2048, 256, 192], P('rep', 'table'), may hold values from -6 to 6
- lc_weight: bfloat16 [256, 256], P('tensor'), may hold values from -0.375 to 0.375
- fm_proj: bfloat16 [256, 256], P(None, 'tensor'), may hold values from -0.375 to 0.375
- fm_out: bfloat16 [256, 192], P('tensor'), may hold values from -0.02734375 to 0.02734375
- cotangent: bfloat16 [2048, 256, 192], P(('rep', 'table')), may hold values from -6 to 6
Outputs:
- layer_out: bfloat16 [2048, 256, 192], P(('rep', 'table'))
- emb_grad: bfloat16 [2048, 256, 192], P('rep', 'table', 'tensor')
- lc_grad: float32 [256, 256], P('tensor')
- proj_grad: float32 [256, 256], P(None, 'tensor')
- out_grad: float32 [256, 192], P('tensor')
All inputs are finite; a program needn't handle non-finite values.
Results may differ from a plain program's by a relative error of at most 0.015.
Values may be sent and summed in bfloat16 or wider, within the bound.
No kernel may reach another device: no remote copies, remote signals or barrier semaphores. Data moves between devices by JAX's collectives and lax.ppermute only.
A program may use at most 32 MiB of HBM per device.

v0:
```python
import jax
import jax.numpy as jnp
from jax import lax
from jax.sharding import PartitionSpec as P


def quarter_terms(embeds, upstream, proj_part, out_part, lc_part, row_start):
    row_count = lc_part.shape[0]
    compressed = jnp.einsum(
        "snd,nk->sdk", embeds, proj_part, preferred_element_type=jnp.float32
    ).astype(jnp.bfloat16)
    interact = jnp.einsum(
        "snd,sdk->snk", embeds, compressed, preferred_element_type=jnp.float32
    ).astype(jnp.bfloat16)
    own_rows = lax.dynamic_slice_in_dim(embeds, row_start, row_count, 1)
    forward_term = jnp.einsum("snk,kd->snd", interact, out_part, preferred_element_type=jnp.float32)
    forward_term = forward_term + jnp.einsum(
        "sjd,jm->smd", own_rows, lc_part, preferred_element_type=jnp.float32
    )
    interact_grad = jnp.einsum(
        "snd,kd->snk", upstream, out_part, preferred_element_type=jnp.float32
    ).astype(jnp.bfloat16)
    compress_grad = jnp.einsum(
        "snd,snk->sdk", embeds, interact_grad, preferred_element_type=jnp.float32
    ).astype(jnp.bfloat16)
    input_grad = jnp.einsum(
        "snk,sdk->snd", interact_grad, compressed, preferred_element_type=jnp.float32
    )
    input_grad = input_grad + jnp.einsum(
        "nk,sdk->snd", proj_part, compress_grad, preferred_element_type=jnp.float32
    )
    lc_rows = jnp.einsum("jm,smd->sjd", lc_part, upstream, preferred_element_type=jnp.float32)
    lc_rows = lc_rows + lax.dynamic_slice_in_dim(upstream, row_start, row_count, 1).astype(
        jnp.float32
    )
    current = lax.dynamic_slice_in_dim(input_grad, row_start, row_count, 1)
    input_grad = lax.dynamic_update_slice_in_dim(input_grad, current + lc_rows, row_start, 1)
    out_term = jnp.einsum("snk,snd->kd", interact, upstream, preferred_element_type=jnp.float32)
    proj_term = jnp.einsum("snd,sdk->nk", embeds, compress_grad, preferred_element_type=jnp.float32)
    lc_term = jnp.einsum("sjd,smd->jm", own_rows, upstream, preferred_element_type=jnp.float32)
    return (forward_term, input_grad, out_term, proj_term, lc_term)


def feed_rows(pooled):
    embeds = lax.all_to_all(pooled, "table", split_axis=0, concat_axis=1, tiled=True)
    return embeds


def shards(pooled, lc_weight, fm_proj, fm_out, cotangent):
    tensor_index = lax.axis_index("tensor")
    table_count = lax.axis_size("table")
    sample_total = cotangent.shape[0] * lax.axis_size("rep") * table_count
    feature_width = cotangent.shape[2]
    emb_count = cotangent.shape[1]
    wide_scale = float(sample_total * feature_width) ** (-0.5)
    out_scale = float(sample_total * emb_count * feature_width) ** (-0.5)
    embeds = feed_rows(pooled)
    row_count = lc_weight.shape[0]
    forward_term, input_grad, out_term, proj_term, lc_term = quarter_terms(
        embeds, cotangent, fm_proj, fm_out, lc_weight, tensor_index * row_count
    )
    mixture = lax.psum(forward_term.astype(jnp.bfloat16), "tensor").astype(jnp.float32)
    layer_out = (embeds.astype(jnp.float32) + mixture).astype(jnp.bfloat16)
    out_grad, proj_grad, lc_grad = lax.psum(
        (out_term * out_scale, proj_term * wide_scale, lc_term * wide_scale), ("rep", "table")
    )
    reduced = lax.psum_scatter(
        input_grad.astype(jnp.bfloat16), "tensor", scatter_dimension=2, tiled=True
    )
    emb_grad = lax.all_to_all(reduced, "table", split_axis=1, concat_axis=0, tiled=True)
    return (layer_out, emb_grad, lc_grad, proj_grad, out_grad)


def solution(mesh):
    in_specs = (
        P("rep", "table", None),
        P("tensor", None),
        P(None, "tensor"),
        P("tensor", None),
        P(("rep", "table"), None, None),
    )
    out_specs = (
        P(("rep", "table"), None, None),
        P("rep", "table", "tensor"),
        P("tensor", None),
        P(None, "tensor"),
        P("tensor", None),
    )
    return jax.shard_map(shards, mesh=mesh, in_specs=in_specs, out_specs=out_specs, check_vma=False)
```

profile of v0, /device:TPU:128, one launch (start us, length us, event | category | flops | bytes accessed | tf_op | source)
XLA Modules:
  0.0 2459.7 jit_solution(4314917212083031155)
XLA Ops:
  7.2 2.7 copy.26
  9.9 26.7 %all-to-all-start = ((bf16[256,8,192]{2,1,0:T(8,128)(2,1)}), bf16[256,8,192]{2,1,0:T(8,128)(2,1)S(1)}, u32[]{:S(2)}, u32[]{:S(2)}) async-start(bf16[256,8,192]{2,1,0:T(8,128)(2,1)} %copy.26), calls=%async_computation | async-start | bytes 2097152 | tf_op jit(solution)/shard_map/all_to_all | solution.py:45
  36.9 96.3 %all-to-all-done = bf16[256,8,192]{2,1,0:T(8,128)(2,1)S(1)} async-done(((bf16[256,8,192]{2,1,0:T(8,128)(2,1)}), bf16[256,8,192]{2,1,0:T(8,128)(2,1)S(1)}, u32[]{:S(2)}, u32[]{:S(2)}) %all-to-all-start) | async-done | bytes 786464 | tf_op jit(solution)/shard_map/all_to_all | solution.py:45
  133.9 0.4 fusion.20
  135.1 1.3 fusion.2
  136.3 9.2 dynamic_update_slice.3
  145.6 1.0 convert_element_type.47
  146.6 0.8 copy-done.6
  147.5 0.4 fusion.3
  147.9 1.6 fusion.14
  149.5 37.7 %reduce-scatter.2.cloned.1.call-done = bf16[8,256,48]{1,2,0:T(8,128)(2,1)} async-done(((bf16[8,256,192]{1,2,0:T(8,128)(2,1)}), bf16[8,256,48]{1,2,0:T(8,128)(2,1)}) %reduce-scatter.2.cloned.1.call-update) | async-done | bytes 196624 | tf_op jit(solution)/shard_map/reduce_scatter | solution.py:67
  187.2 2.0 copy.33
  189.2 2.5 reshape.16
  191.7 20.7 all-to-all-start.1
  212.5 2.7 fusion
  215.3 1.3 copy.28
  216.6 0.9 fusion.6
  217.5 1.1 fusion.8
  219.0 2226.5 %psum.31 = f32[64,192]{1,0:T(8,128)} all-reduce(f32[64,192]{1,0:T(8,128)S(1)} %fusion.5), channel_id=1, replica_groups=mesh['rep'=8,'table'=32,'tensor'=4] {'rep','table'}, use_global_device_ids=true, to_apply=%region_4.0 | all-reduce | flops 12288 | bytes 98304 | tf_op jit(solution)/shard_map/psum | solution.py:64
  2445.5 2.2 add_convert_fusion
  2447.7 1.4 reshape.17
  2449.3 1.0 copy.37
  2450.3 1.5 copy.54
  2451.7 1.5 copy.55
  (33 shorter events, 2.3 us)
Async XLA Ops:
  7.2 29.4 %copy-start = (bf16[64,192]{1,0:T(8,128)(2,1)S(1)}, bf16[64,192]{1,0:T(8,128)(2,1)}, u32[]{:S(2)}) copy-start(bf16[64,192]{1,0:T(8,128)(2,1)} %param.8) | copy-start | bytes 73732
  7.2 29.4 %copy-start.1 = (bf16[8,256,192]{1,2,0:T(8,128)(2,1)S(1)}, bf16[8,256,192]{1,2,0:T(8,128)(2,1)}, u32[]{:S(2)}) copy-start(bf16[8,256,192]{1,2,0:T(8,128)(2,1)} %param.9) | copy-start | bytes 2359300
  9.9 123.4 %copy-start.7 = (bf16[256,64]{0,1:T(8,128)(2,1)S(1)}, bf16[256,64]{0,1:T(8,128)(2,1)}, u32[]{:S(2)}) copy-start(bf16[256,64]{0,1:T(8,128)(2,1)} %param.7) | copy-start | bytes 98308
  9.9 123.4 %all-to-all-start = ((bf16[256,8,192]{2,1,0:T(8,128)(2,1)}), bf16[256,8,192]{2,1,0:T(8,128)(2,1)S(1)}, u32[]{:S(2)}, u32[]{:S(2)}) async-start(bf16[256,8,192]{2,1,0:T(8,128)(2,1)} %copy.26), calls=%async_computation | async-start | bytes 2097152 | tf_op jit(solution)/shard_map/all_to_all | solution.py:45
  36.6 150.7 %reduce-scatter.2.cloned.1.call-start = ((), (), s32[]{:S(2)}) async-start(), calls=%async_computation.4 | async-start | bytes 983040 | tf_op jit(solution)/shard_map/reduce_scatter | solution.py:67
  133.5 0.7 copy-start.5
  133.9 0.9 copy-start.3
  134.3 0.8 copy-start.8
  146.5 0.9 copy-start.6
  191.7 2256.0 %all-to-all-start.1 = ((bf16[32,2,1536]{2,1,0:T(2,128)(2,1)}), bf16[32,2,1536]{2,1,0:T(2,128)(2,1)}, u32[]{:S(2)}, u32[]{:S(2)}) async-start(bf16[32,2,1536]{2,1,0:T(2,128)(2,1)} %reshape.16), calls=%async_computation.2 | async-start | bytes 393216 | tf_op jit(solution)/shard_map/all_to_all | solution.py:70
  212.5 2233.1 %all-reduce.4.cloned.1.call-start = ((), (), s32[]{:S(2)}) async-start(), calls=%async_computation.3 | async-start | bytes 1572864 | tf_op jit(solution)/shard_map/psum | solution.py:62
  215.2 2.3 copy-start.4
  215.2 2235.0 %all-reduce.6.cloned.1.call-start = ((), (), s32[]{:S(2)}) async-start(), calls=%async_computation.5 | async-start | bytes 262144 | tf_op jit(solution)/shard_map/psum | solution.py:64
  217.5 2228.0 %copy-start.2 = (bf16[8,256,192]{1,2,0:T(8,128)(2,1)S(1)}, bf16[8,256,192]{1,2,0:T(8,128)(2,1)}, u32[]{:S(2)}) copy-start(bf16[8,256,192]{1,2,0:T(8,128)(2,1)} %copy.28) | copy-start | bytes 2359300
Sparse Core Ops, SparseCore 0:
  146.7 40.5 reduce-scatter.1
  216.2 83.7 all-reduce.3
  304.1 607.0 all-reduce.5
where the time goes:
time: 2460 us
  blocking collectives  2230 us (91%)
  waiting for transfers between devices  134 us (5%)
  starting transfers between devices  47.5 us (2%)
    psum x1, blocking collectives, shards(): lax.psum((out_term * out_scale, proj_term * wide_scale, lc_term * wide_sc...  2230 us
    all_to_all x1, waiting for transfers between devices, feed_rows(): lax.all_to_all(pooled, 'table', split_axis=0, concat_axis=1, tiled=True)  96.3 us
  transfers between devices with their start and end apart: 5, of which 2 were waited for; matrix products, arithmetic and copies ran while one was open for 1% of the time, Pallas kernels for 0%

commit v1 on v0

v1 whole, which is shorter than its diff:
```python
import jax
import jax.numpy as jnp
from jax import lax
from jax.experimental import pallas as pl
from jax.experimental.pallas import tpu as pltpu
from jax.sharding import Mesh, PartitionSpec as P

BF = jnp.bfloat16
F32 = jnp.float32
TABLE = ("zhi", "y", "core")
PLANE = ("y", "core", "x")
COLUMN = ("y", "core")
VMEM_BYTES = 48 * 1024 * 1024


def dot(a, b):
    return lax.dot_general(a, b, (((1,), (0,)), ((), ())), preferred_element_type=F32)


def dot_t(a, b):
    return lax.dot_general(a, b, (((1,), (1,)), ((), ())), preferred_element_type=F32)


def params():
    return pltpu.CompilerParams(vmem_limit_bytes=VMEM_BYTES)


def whole(shape):
    zeros = (0,) * len(shape)
    return pl.BlockSpec(shape, lambda i, t: zeros)


def pack_kernel(t_ref, pooled_ref, out_ref):
    first = pooled_ref[:, 0, 0].astype(F32)
    second = pooled_ref[:, 0, 1].astype(F32)
    n = first.shape[0]
    mixed = jnp.concatenate([first[:, :, 128:], second[:, :, 128:]], axis=2)
    rows = jnp.concatenate([first[:, :, :128], second[:, :, :128], mixed], axis=1)
    out_ref[...] = rows.astype(BF).reshape(n, 24, 128)


def pack_rows(t, pooled):
    view = pooled.reshape(32, 4, 2, 8, 192)
    return pl.pallas_call(
        pack_kernel,
        grid_spec=pltpu.PrefetchScalarGridSpec(
            num_scalar_prefetch=1,
            grid=(1,),
            in_specs=[pl.BlockSpec((32, 1, 2, 8, 192), lambda i, t: (0, t[0], 0, 0, 0))],
            out_specs=whole((32, 24, 128)),
        ),
        out_shape=jax.ShapeDtypeStruct((32, 24, 128), BF),
        compiler_params=params(),
        name="pack_rows",
    )(t, view)


def upstream_kernel(t_ref, g_ref, w_ref, ig_ref, igt_ref, base_ref, wt_ref, p_ref):
    lc = w_ref[:, :256]
    pt = w_ref[:, 256:512]
    out_w = w_ref[:, 512:704]
    wt_ref[...] = lc.astype(F32).T.astype(BF)
    p_ref[...] = pt.astype(F32).T.astype(BF)
    for s in range(2):
        g = g_ref[s]
        ig_ref[s] = dot_t(g, out_w).astype(BF)
        igt_ref[s] = dot_t(out_w, g).astype(BF)
        base_ref[s] = g.astype(F32) + dot(lc, g)


def upstream_terms(t, cotangent, weights):
    return pl.pallas_call(
        upstream_kernel,
        grid_spec=pltpu.PrefetchScalarGridSpec(
            num_scalar_prefetch=1,
            grid=(1,),
            in_specs=[
                pl.BlockSpec((2, 256, 192), lambda i, t: (t[0], 0, 0)),
                whole((256, 704)),
            ],
            out_specs=[
                whole((2, 256, 256)),
                whole((2, 256, 256)),
                whole((2, 256, 192)),
                whole((256, 256)),
                whole((256, 256)),
            ],
        ),
        out_shape=[
            jax.ShapeDtypeStruct((2, 256, 256), BF),
            jax.ShapeDtypeStruct((2, 256, 256), BF),
            jax.ShapeDtypeStruct((2, 256, 192), F32),
            jax.ShapeDtypeStruct((256, 256), BF),
            jax.ShapeDtypeStruct((256, 256), BF),
        ],
        compiler_params=params(),
        name="upstream_terms",
    )(t, cotangent, weights)


def layer_kernel(t_ref, x_ref, g_ref, w_ref, ig_ref, igt_ref, base_ref, wt_ref, p_ref, layer_ref, msg_ref):
    pt = w_ref[:, 256:512]
    out_w = w_ref[:, 512:704]
    wt = wt_ref[...]
    planes = x_ref[...].astype(F32)
    plane = [planes[:, 8 * i : 8 * i + 8].reshape(256, 128) for i in range(3)]
    xs = [
        jnp.concatenate([plane[0], plane[2][:, :64]], axis=1),
        jnp.concatenate([plane[1], plane[2][:, 64:]], axis=1),
    ]
    grads = []
    out_sum = proj_sum = lc_sum = None
    for s in range(2):
        x32 = xs[s]
        x = x32.astype(BF)
        g = g_ref[s]
        ct = dot(pt, x).astype(BF)
        inter = dot_t(x, ct).astype(BF)
        inter_t = dot_t(ct, x).astype(BF)
        forward = dot(inter, out_w) + dot(wt, x)
        layer_ref[s] = (x32 + forward).astype(BF)
        cgt = dot(igt_ref[s], x).astype(BF)
        grads.append(base_ref[s] + dot(ig_ref[s], ct) + dot(p_ref[...], cgt))
        out_term, proj_term, lc_term = dot(inter_t, g), dot_t(cgt, x), dot_t(x, g)
        out_sum = out_term if s == 0 else out_sum + out_term
        proj_sum = proj_term if s == 0 else proj_sum + proj_term
        lc_sum = lc_term if s == 0 else lc_sum + lc_term
    pad = jnp.zeros((256, 32), F32)
    emb = [
        jnp.concatenate([grads[0][:, 48 * q : 48 * q + 48], grads[1][:, 48 * q : 48 * q + 48], pad], axis=1)
        for q in range(4)
    ]
    out_tail = jnp.concatenate([out_sum[:, 128:], jnp.zeros((256, 64), F32)], axis=1)
    for c in range(8):
        for q in range(4):
            rows = slice(64 * q + 8 * c, 64 * q + 8 * c + 8)
            tiles = [emb[q][64 * z + 8 * c : 64 * z + 8 * c + 8] for z in range(4)]
            tiles += [lc_sum[rows, :128], lc_sum[rows, 128:]]
            tiles += [proj_sum[rows, :128], proj_sum[rows, 128:]]
            tiles += [out_sum[rows, :128], out_tail[rows]]
            msg_ref[4 * c + q] = jnp.concatenate(tiles, axis=0).astype(BF)


def layer_terms(t, rows, cotangent, weights, ig, igt, base, wt, p):
    return pl.pallas_call(
        layer_kernel,
        grid_spec=pltpu.PrefetchScalarGridSpec(
            num_scalar_prefetch=1,
            grid=(1,),
            in_specs=[
                whole((32, 24, 128)),
                pl.BlockSpec((2, 256, 192), lambda i, t: (t[0], 0, 0)),
                whole((256, 704)),
                whole((2, 256, 256)),
                whole((2, 256, 256)),
                whole((2, 256, 192)),
                whole((256, 256)),
                whole((256, 256)),
            ],
            out_specs=[whole((2, 256, 192)), whole((32, 80, 128))],
        ),
        out_shape=[
            jax.ShapeDtypeStruct((2, 256, 192), BF),
            jax.ShapeDtypeStruct((32, 80, 128), BF),
        ],
        compiler_params=params(),
        name="layer_terms",
    )(t, rows, cotangent, weights, ig, igt, base, wt, p)


def plane_kernel(in_ref, out_ref):
    total = in_ref[0, 32:80].astype(F32)
    for d in range(1, 32):
        total = total + in_ref[d, 32:80].astype(F32)
    total = total.astype(BF)
    wide = []
    for c in range(8):
        parts = [in_ref[4 * c + q, 0:32].astype(F32)[:, :96] for q in range(4)]
        wide.append(jnp.concatenate(parts, axis=1))
    for z in range(4):
        rows = jnp.concatenate([wide[c][8 * z : 8 * z + 8] for c in range(8)], axis=0).astype(BF)
        for i in range(3):
            out_ref[z, 64 * i : 64 * i + 64] = rows[:, 128 * i : 128 * i + 128]
        out_ref[z, 192:240] = total


def plane_terms(received):
    return pl.pallas_call(
        plane_kernel,
        out_shape=jax.ShapeDtypeStruct((4, 240, 128), BF),
        compiler_params=params(),
        name="plane_terms",
    )(received)


def column_kernel(in_ref, emb_ref, total_ref):
    total = in_ref[0, 192:240].astype(F32)
    for z in range(1, 4):
        total = total + in_ref[z, 192:240].astype(F32)
    total_ref[...] = total
    for z in range(4):
        planes = [in_ref[z, 64 * i : 64 * i + 64].astype(F32) for i in range(3)]
        rows = jnp.concatenate(planes, axis=1).reshape(8, 8, 384)
        for i in range(8):
            emb_ref[8 * z : 8 * z + 8, i] = rows[:, :, 48 * i : 48 * i + 48].astype(BF)


def column_terms(received):
    return pl.pallas_call(
        column_kernel,
        out_shape=[
            jax.ShapeDtypeStruct((32, 8, 8, 48), BF),
            jax.ShapeDtypeStruct((48, 128), F32),
        ],
        compiler_params=params(),
        name="column_terms",
    )(received)


def final_kernel(wide_scale, out_scale, in_ref, lc_ref, proj_ref, out_ref):
    rows = [in_ref[c] for c in range(8)]
    part = [jnp.concatenate([r[8 * i : 8 * i + 8] for r in rows], axis=0) for i in range(6)]
    lc_ref[...] = jnp.concatenate(part[0:2], axis=1) * wide_scale
    proj_ref[...] = jnp.concatenate([part[2].T, part[3].T], axis=0) * wide_scale
    out_ref[...] = jnp.concatenate([part[4], part[5][:, :64]], axis=1) * out_scale


def final_terms(received, wide_scale, out_scale):
    def kernel(*refs):
        final_kernel(wide_scale, out_scale, *refs)

    return pl.pallas_call(
        kernel,
        out_shape=[
            jax.ShapeDtypeStruct((64, 256), F32),
            jax.ShapeDtypeStruct((256, 64), F32),
            jax.ShapeDtypeStruct((64, 192), F32),
        ],
        compiler_params=params(),
        name="final_terms",
    )(received)


def spread(block, axes, count):
    copies = jnp.broadcast_to(block[None], (count,) + block.shape)
    return lax.all_to_all(copies, axes, split_axis=0, concat_axis=0, tiled=True)


def shards(pooled, lc_weight, fm_proj, fm_out, cotangent):
    t = lax.axis_index("x").astype(jnp.int32)[None]
    rep_count = lax.axis_size("zlo")
    sample_total = cotangent.shape[0] * rep_count * 32
    wide_scale = float(sample_total * 192) ** (-0.5)
    out_scale = float(sample_total * 256 * 192) ** (-0.5)
    sent = pack_rows(t, pooled)
    rows = lax.all_to_all(sent, TABLE, split_axis=0, concat_axis=0, tiled=True)
    own = jnp.concatenate([lc_weight, fm_proj.T, fm_out], axis=1)
    weights = spread(own, "x", 4).reshape(256, 704)
    ig, igt, base, wt, p = upstream_terms(t, cotangent, weights)
    layer, messages = layer_terms(t, rows, cotangent, weights, ig, igt, base, wt, p)
    plane = lax.all_to_all(messages, PLANE, split_axis=0, concat_axis=0, tiled=True)
    column = plane_terms(plane)
    column = lax.all_to_all(column, "zhi", split_axis=0, concat_axis=0, tiled=True)
    emb_grad, total = column_terms(column)
    total = jnp.sum(spread(total, "zlo", rep_count), axis=0)
    lc_grad, proj_grad, out_grad = final_terms(spread(total, COLUMN, 8), wide_scale, out_scale)
    layer_out = spread(layer, "x", 4).reshape(8, 256, 192)
    return (layer_out, emb_grad.reshape(256, 8, 48), lc_grad, proj_grad, out_grad)


def solution(mesh):
    reps = mesh.shape["rep"]
    fine = Mesh(mesh.devices.reshape(reps, 4, 4, 2, 4), ("zlo", "zhi", "y", "core", "x"))
    in_specs = (
        P("zlo", TABLE, None),
        P("x", None),
        P(None, "x"),
        P("x", None),
        P(("zlo",) + TABLE, None, None),
    )
    out_specs = (
        P(("zlo",) + TABLE, None, None),
        P("zlo", TABLE, "x"),
        P("x", None),
        P(None, "x"),
        P("x", None),
    )
    return jax.shard_map(shards, mesh=fine, in_specs=in_specs, out_specs=out_specs, check_vma=False)
```

time: 2460 us -> 192 us (0.08)
  the two profiles are of different devices: /device:TPU:128 before, /device:TPU:1 now
where the time goes in v1:
time: 192 us
  starting transfers between devices  65.7 us (34%)
  waiting for transfers between devices  61.2 us (32%)
  blocking collectives  52.5 us (27%)
  local copies, waits for them, and re-layouts  7.29 us (4%)
  Pallas kernels  3.49 us (2%)
    all_to_all x1, blocking collectives, shards(): lax.all_to_all(column, 'zhi', split_axis=0, concat_axis=0, tiled=True)  36.5 us
    all_to_all x1, starting transfers between devices, shards(): rows = lax.all_to_all(sent, TABLE, split_axis=0, concat_axis=0, tiled=True)  33.9 us
    all_to_all x1, waiting for transfers between devices, shards(): rows = lax.all_to_all(sent, TABLE, split_axis=0, concat_axis=0, tiled=True)  32.4 us
    all_to_all x4, starting transfers between devices, spread(): return lax.all_to_all(copies, axes, split_axis=0, concat_axis=0, tiled=True)  31.7 us
    all_to_all x4, waiting for transfers between devices, spread(): return lax.all_to_all(copies, axes, split_axis=0, concat_axis=0, tiled=True)  28.8 us
    all_to_all x1, blocking collectives, shards(): lax.all_to_all(messages, PLANE, split_axis=0, concat_axis=0, tiled=True)  16.1 us
    unnamed x9, local copies, waits for them, and re-layouts  4.07 us
  transfers between devices with their start and end apart: 5, of which 5 were waited for; matrix products, arithmetic and copies ran while one was open for 1% of the time, Pallas kernels for 1%

profile of v1, /device:TPU:1, one launch (start us, length us, event | category | flops | bytes accessed | tf_op | source)
XLA Modules:
  0.0 191.8 jit_solution(12056526634416808417)
XLA Ops:
  0.6 0.9 pad_maximum_fusion
  1.5 0.8 broadcast_in_dim.11
  2.3 4.8 %all-to-all-start.1 = ((bf16[4,64,704]{2,1,0:T(8,128)(2,1)}), bf16[4,64,704]{2,1,0:T(8,128)(2,1)S(1)}, u32[]{:S(2)}, u32[]{:S(2)}) async-start(bf16[4,64,704]{2,1,0:T(8,128)(2,1)} %broadcast_in_dim.11), calls=%async_computation.1 | async-start | bytes 786432 | tf_op jit(solution)/shard_map/all_to_all | solution.py:246
  7.1 1.0 copy.16
  8.1 0.8 pack_rows.1
  8.9 4.5 %all-to-all-done.1 = bf16[4,64,704]{2,1,0:T(8,128)(2,1)S(1)} async-done(((bf16[4,64,704]{2,1,0:T(8,128)(2,1)}), bf16[4,64,704]{2,1,0:T(8,128)(2,1)S(1)}, u32[]{:S(2)}, u32[]{:S(2)}) %all-to-all-start.1) | async-done | bytes 360480 | tf_op jit(solution)/shard_map/all_to_all | solution.py:246
  13.4 33.9 %all-to-all-start = ((bf16[32,24,128]{2,1,0:T(8,128)(2,1)}), bf16[32,24,128]{2,1,0:T(8,128)(2,1)S(1)}, u32[]{:S(2)}, u32[]{:S(2)}) async-start(bf16[32,24,128]{2,1,0:T(8,128)(2,1)} %pack_rows.1), calls=%async_computation | async-start | bytes 393216 | tf_op jit(solution)/shard_map/all_to_all | solution.py:256
  48.2 32.4 %all-to-all-done.x_ref = bf16[32,24,128]{2,1,0:T(8,128)(2,1)S(1)} async-done(((bf16[32,24,128]{2,1,0:T(8,128)(2,1)}), bf16[32,24,128]{2,1,0:T(8,128)(2,1)S(1)}, u32[]{:S(2)}, u32[]{:S(2)}) %all-to-all-start) | async-done | bytes 196640 | tf_op jit(solution)/shard_map/all_to_all | solution.py:256
  80.7 1.2 layer_terms.1
  81.9 16.1 %all_to_all.35.in_ref = bf16[32,80,128]{2,1,0:T(8,128)(2,1)S(1)} all-to-all(bf16[32,80,128]{2,1,0:T(8,128)(2,1)S(1)} %get-tuple-element.23), channel_id=1, replica_groups=mesh['zlo'=8,'zhi'=4,'y'=4,'core'=2,'x'=4] {'y','core','x'}, dimensions={0} | all-to-all | bytes 1310720 | tf_op jit(solution)/shard_map/all_to_all | solution.py:261
  98.1 36.5 %all_to_all.36.in_ref = bf16[4,240,128]{2,1,0:T(8,128)(2,1)S(1)} all-to-all(bf16[4,240,128]{2,1,0:T(8,128)(2,1)S(1)} %plane_terms.1), channel_id=1, replica_groups=mesh['zlo'=8,'zhi'=4,'y'=4,'core'=2,'x'=4] {'zhi'}, dimensions={0} | all-to-all | bytes 491520 | tf_op jit(solution)/shard_map/all_to_all | solution.py:263
  134.8 0.7 broadcast_in_dim.13
  135.5 15.3 %all-to-all-start.5 = ((f32[8,48,128]{2,1,0:T(8,128)}), f32[8,48,128]{2,1,0:T(8,128)S(1)}, u32[]{:S(2)}, u32[]{:S(2)}) async-start(f32[8,48,128]{2,1,0:T(8,128)} %broadcast_in_dim.13), calls=%async_computation.5 | async-start | bytes 393216 | tf_op jit(solution)/shard_map/all_to_all | solution.py:246
  150.9 11.1 %all-to-all-done.5 = f32[8,48,128]{2,1,0:T(8,128)S(1)} async-done(((f32[8,48,128]{2,1,0:T(8,128)}), f32[8,48,128]{2,1,0:T(8,128)S(1)}, u32[]{:S(2)}, u32[]{:S(2)}) %all-to-all-start.5) | async-done | bytes 196640 | tf_op jit(solution)/shard_map/all_to_all | solution.py:246
  162.0 0.9 broadcast_in_dim.12
  162.9 3.5 %all-to-all-start.2 = ((bf16[4,2,256,192]{2,3,1,0:T(8,128)(2,1)}), bf16[4,2,256,192]{2,3,1,0:T(8,128)(2,1)S(1)}, u32[]{:S(2)}, u32[]{:S(2)}) async-start(bf16[4,2,256,192]{2,3,1,0:T(8,128)(2,1)} %broadcast_in_dim.12), calls=%async_computation.2 | async-start | bytes 1572864 | tf_op jit(solution)/shard_map/all_to_all | solution.py:246
  166.4 8.3 %all-to-all-done.2 = bf16[4,2,256,192]{2,3,1,0:T(8,128)(2,1)S(1)} async-done(((bf16[4,2,256,192]{2,3,1,0:T(8,128)(2,1)}), bf16[4,2,256,192]{2,3,1,0:T(8,128)(2,1)S(1)}, u32[]{:S(2)}, u32[]{:S(2)}) %all-to-all-start.2) | async-done | bytes 786464 | tf_op jit(solution)/shard_map/all_to_all | solution.py:246
  174.8 0.7 broadcast_in_dim.14
  175.5 8.2 %all-to-all-start.6 = ((f32[8,48,128]{2,1,0:T(8,128)}), f32[8,48,128]{2,1,0:T(8,128)S(1)}, u32[]{:S(2)}, u32[]{:S(2)}) async-start(f32[8,48,128]{2,1,0:T(8,128)} %broadcast_in_dim.14), calls=%async_computation.6 | async-start | bytes 393216 | tf_op jit(solution)/shard_map/all_to_all | solution.py:246
  183.6 1.0 copy.20
  184.6 4.9 %all-to-all-done.6.refs_0_ = f32[8,48,128]{2,1,0:T(8,128)S(1)} async-done(((f32[8,48,128]{2,1,0:T(8,128)}), f32[8,48,128]{2,1,0:T(8,128)S(1)}, u32[]{:S(2)}, u32[]{:S(2)}) %all-to-all-start.6) | async-done | bytes 196640 | tf_op jit(solution)/shard_map/all_to_all | solution.py:246
  189.5 0.7 final_terms.1
  190.2 0.7 copy.21
  190.9 0.9 copy.23
  (10 shorter events, 1.5 us)
Async XLA Ops:
  0.6 6.5 %copy-start = (bf16[256,8,192]{0,2,1:T(8,128)(2,1)S(1)}, bf16[256,8,192]{0,2,1:T(8,128)(2,1)}, u32[]{:S(2)}) copy-start(bf16[256,8,192]{0,2,1:T(8,128)(2,1)} %param.5) | copy-start | bytes 2359300
  2.3 11.1 %all-to-all-start.1 = ((bf16[4,64,704]{2,1,0:T(8,128)(2,1)}), bf16[4,64,704]{2,1,0:T(8,128)(2,1)S(1)}, u32[]{:S(2)}, u32[]{:S(2)}) async-start(bf16[4,64,704]{2,1,0:T(8,128)(2,1)} %broadcast_in_dim.11), calls=%async_computation.1 | async-start | bytes 786432 | tf_op jit(solution)/shard_map/all_to_all | solution.py:246
  8.1 39.2 %copy-start.1 = (bf16[8,256,192]{1,2,0:T(8,128)(2,1)S(1)}, bf16[8,256,192]{1,2,0:T(8,128)(2,1)}, u32[]{:S(2)}) copy-start(bf16[8,256,192]{1,2,0:T(8,128)(2,1)} %param.9) | copy-start | bytes 2359300
  13.4 67.3 %all-to-all-start = ((bf16[32,24,128]{2,1,0:T(8,128)(2,1)}), bf16[32,24,128]{2,1,0:T(8,128)(2,1)S(1)}, u32[]{:S(2)}, u32[]{:S(2)}) async-start(bf16[32,24,128]{2,1,0:T(8,128)(2,1)} %pack_rows.1), calls=%async_computation | async-start | bytes 393216 | tf_op jit(solution)/shard_map/all_to_all | solution.py:256
  135.5 26.5 %all-to-all-start.5 = ((f32[8,48,128]{2,1,0:T(8,128)}), f32[8,48,128]{2,1,0:T(8,128)S(1)}, u32[]{:S(2)}, u32[]{:S(2)}) async-start(f32[8,48,128]{2,1,0:T(8,128)} %broadcast_in_dim.13), calls=%async_computation.5 | async-start | bytes 393216 | tf_op jit(solution)/shard_map/all_to_all | solution.py:246
  162.9 11.8 %all-to-all-start.2 = ((bf16[4,2,256,192]{2,3,1,0:T(8,128)(2,1)}), bf16[4,2,256,192]{2,3,1,0:T(8,128)(2,1)S(1)}, u32[]{:S(2)}, u32[]{:S(2)}) async-start(bf16[4,2,256,192]{2,3,1,0:T(8,128)(2,1)} %broadcast_in_dim.12), calls=%async_computation.2 | async-start | bytes 1572864 | tf_op jit(solution)/shard_map/all_to_all | solution.py:246
  175.5 14.1 %all-to-all-start.6 = ((f32[8,48,128]{2,1,0:T(8,128)}), f32[8,48,128]{2,1,0:T(8,128)S(1)}, u32[]{:S(2)}, u32[]{:S(2)}) async-start(f32[8,48,128]{2,1,0:T(8,128)} %broadcast_in_dim.14), calls=%async_computation.6 | async-start | bytes 393216 | tf_op jit(solution)/shard_map/all_to_all | solution.py:246

commit v2 on v1

--- a/solution.py
+++ b/solution.py
@@ -197,7 +197,8 @@
     total = in_ref[0, 192:240].astype(F32)
     for z in range(1, 4):
         total = total + in_ref[z, 192:240].astype(F32)
-    total_ref[...] = total
+    for r in range(total_ref.shape[0]):
+        total_ref[r] = total.astype(BF)
     for z in range(4):
         planes = [in_ref[z, 64 * i : 64 * i + 64].astype(F32) for i in range(3)]
         rows = jnp.concatenate(planes, axis=1).reshape(8, 8, 384)
@@ -205,15 +206,32 @@
             emb_ref[8 * z : 8 * z + 8, i] = rows[:, :, 48 * i : 48 * i + 48].astype(BF)
 
 
-def column_terms(received):
+def column_terms(received, rep_count):
     return pl.pallas_call(
         column_kernel,
         out_shape=[
             jax.ShapeDtypeStruct((32, 8, 8, 48), BF),
-            jax.ShapeDtypeStruct((48, 128), F32),
+            jax.ShapeDtypeStruct((rep_count, 48, 128), BF),
         ],
         compiler_params=params(),
         name="column_terms",
+    )(received)
+
+
+def replica_kernel(in_ref, out_ref):
+    total = in_ref[0].astype(F32)
+    for r in range(1, in_ref.shape[0]):
+        total = total + in_ref[r].astype(F32)
+    for c in range(8):
+        out_ref[c] = total
+
+
+def replica_terms(received):
+    return pl.pallas_call(
+        replica_kernel,
+        out_shape=jax.ShapeDtypeStruct((8, 48, 128), F32),
+        compiler_params=params(),
+        name="replica_terms",
     )(received)
 
 
@@ -221,7 +239,7 @@
     rows = [in_ref[c] for c in range(8)]
     part = [jnp.concatenate([r[8 * i : 8 * i + 8] for r in rows], axis=0) for i in range(6)]
     lc_ref[...] = jnp.concatenate(part[0:2], axis=1) * wide_scale
-    proj_ref[...] = jnp.concatenate([part[2].T, part[3].T], axis=0) * wide_scale
+    proj_ref[...] = jnp.concatenate(part[2:4], axis=1) * wide_scale
     out_ref[...] = jnp.concatenate([part[4], part[5][:, :64]], axis=1) * out_scale
 
 
@@ -233,7 +251,7 @@
         kernel,
         out_shape=[
             jax.ShapeDtypeStruct((64, 256), F32),
-            jax.ShapeDtypeStruct((256, 64), F32),
+            jax.ShapeDtypeStruct((64, 256), F32),
             jax.ShapeDtypeStruct((64, 192), F32),
         ],
         compiler_params=params(),
@@ -241,9 +259,8 @@
     )(received)
 
 
-def spread(block, axes, count):
-    copies = jnp.broadcast_to(block[None], (count,) + block.shape)
-    return lax.all_to_all(copies, axes, split_axis=0, concat_axis=0, tiled=True)
+def swap(blocks, axes):
+    return lax.all_to_all(blocks, axes, split_axis=0, concat_axis=0, tiled=True)
 
 
 def shards(pooled, lc_weight, fm_proj, fm_out, cotangent):
@@ -252,20 +269,19 @@
     sample_total = cotangent.shape[0] * rep_count * 32
     wide_scale = float(sample_total * 192) ** (-0.5)
     out_scale = float(sample_total * 256 * 192) ** (-0.5)
-    sent = pack_rows(t, pooled)
-    rows = lax.all_to_all(sent, TABLE, split_axis=0, concat_axis=0, tiled=True)
+    rows = swap(pack_rows(t, pooled), TABLE)
     own = jnp.concatenate([lc_weight, fm_proj.T, fm_out], axis=1)
-    weights = spread(own, "x", 4).reshape(256, 704)
+    weights = lax.all_gather(own, "x", axis=0, tiled=True)
     ig, igt, base, wt, p = upstream_terms(t, cotangent, weights)
     layer, messages = layer_terms(t, rows, cotangent, weights, ig, igt, base, wt, p)
-    plane = lax.all_to_all(messages, PLANE, split_axis=0, concat_axis=0, tiled=True)
-    column = plane_terms(plane)
-    column = lax.all_to_all(column, "zhi", split_axis=0, concat_axis=0, tiled=True)
-    emb_grad, total = column_terms(column)
-    total = jnp.sum(spread(total, "zlo", rep_count), axis=0)
-    lc_grad, proj_grad, out_grad = final_terms(spread(total, COLUMN, 8), wide_scale, out_scale)
-    layer_out = spread(layer, "x", 4).reshape(8, 256, 192)
-    return (layer_out, emb_grad.reshape(256, 8, 48), lc_grad, proj_grad, out_grad)
+    plane = plane_terms(swap(messages, PLANE))
+    column = swap(plane, "zhi")
+    layer_out = lax.all_gather(layer, "x", axis=0, tiled=True)
+    column, _ = lax.optimization_barrier((column, layer_out))
+    emb_grad, total = column_terms(column, rep_count)
+    total = replica_terms(swap(total, "zlo"))
+    lc_grad, proj_grad, out_grad = final_terms(swap(total, COLUMN), wide_scale, out_scale)
+    return (layer_out, emb_grad.reshape(256, 8, 48), lc_grad, proj_grad.T, out_grad)
 
 
 def solution(mesh):

time: 192 us -> 165 us (0.86)
  starting transfers between devices: 65.7 us -> 47.6 us
  waiting for transfers between devices: 61.2 us -> 44.3 us
  blocking collectives: 52.5 us -> 62.1 us
  local copies, waits for them, and re-layouts: 7.29 us -> 4.59 us
    all_gather x0 -> x2, blocking collectives: none -> 21.8 us  [the longest x1 11.1 us: shards(): layer_out = lax.all_gather(layer, 'x', axis=0, tiled=True)]
    all_to_all x5 -> x3, starting transfers between devices: 65.7 us -> 47.6 us  [swap(): return lax.all_to_all(blocks, axes, split_axis=0, concat_axis=0, tiled=True)]
    all_to_all x5 -> x3, waiting for transfers between devices: 61.2 us -> 44.3 us  [swap(): return lax.all_to_all(blocks, axes, split_axis=0, concat_axis=0, tiled=True)]
    all_to_all x2, blocking collectives: 52.5 us -> 40.3 us  [swap(): return lax.all_to_all(blocks, axes, split_axis=0, concat_axis=0, tiled=True)]
    broadcast_in_dim x4 -> x0, local copies, waits for them, and re-layouts: 3.09 us -> none  [spread(): copies = jnp.broadcast_to(block[None], (count,) + block.shape)]
    unnamed x9 -> x12, local copies, waits for them, and re-layouts: 4.07 us -> 4.46 us
  transfers between devices with their start and end apart: 5 -> 3, of which waited for: 5 -> 3; matrix products, arithmetic and copies ran while one was open for 1% -> 1% of each run, Pallas kernels for 1% -> 0%
where the time goes in v2:
time: 165 us; the launch traced here: 164 us
  blocking collectives  62.1 us (38%)
  starting transfers between devices  47.6 us (29%)
  waiting for transfers between devices  44.3 us (27%)
  Pallas kernels  4.9 us (3%)
  local copies, waits for them, and re-layouts  4.59 us (3%)
    all_to_all x3, starting transfers between devices, swap(): return lax.all_to_all(blocks, axes, split_axis=0, concat_axis=0, tiled=True)  47.6 us
    all_to_all x3, waiting for transfers between devices, swap(): return lax.all_to_all(blocks, axes, split_axis=0, concat_axis=0, tiled=True)  44.3 us
    all_to_all x2, blocking collectives, swap(): return lax.all_to_all(blocks, axes, split_axis=0, concat_axis=0, tiled=True)  40.3 us
    all_gather x1, blocking collectives, shards(): layer_out = lax.all_gather(layer, 'x', axis=0, tiled=True)  11.1 us
    all_gather x1, blocking collectives, shards(): weights = lax.all_gather(own, 'x', axis=0, tiled=True)  10.7 us
    unnamed x12, local copies, waits for them, and re-layouts  4.46 us
  transfers between devices with their start and end apart: 3, of which 3 were waited for; matrix products, arithmetic and copies ran while one was open for 1% of the time, Pallas kernels for 0%

profile of v2, /device:TPU:1, one launch (start us, length us, event | category | flops | bytes accessed | tf_op | source)
XLA Modules:
  0.0 164.2 jit_solution(9427372486737363607)
XLA Ops:
  0.6 1.8 %copy.15 = bf16[256,8,192]{2,1,0:T(8,128)(2,1)S(1)} copy(bf16[256,8,192]{0,2,1:T(8,128)(2,1)} %param.5) | data formatting | bytes 1572864 | tf_op args[0]
  2.5 0.8 pack_rows.1
  3.2 32.6 %all-to-all-start = ((bf16[32,24,128]{2,1,0:T(8,128)(2,1)}), bf16[32,24,128]{2,1,0:T(8,128)(2,1)S(1)}, u32[]{:S(2)}, u32[]{:S(2)}) async-start(bf16[32,24,128]{2,1,0:T(8,128)(2,1)} %pack_rows.1), calls=%async_computation | async-start | bytes 393216 | tf_op jit(solution)/shard_map/all_to_all | solution.py:263
  35.9 0.5 copy.17.g_ref
  36.4 0.2 copy-done.1
  36.6 0.0 copy-done.2
  36.7 10.7 %all_gather.6.w_ref = bf16[256,704]{1,0:T(8,128)(2,1)S(1)} all-gather(bf16[64,704]{1,0:T(8,128)(2,1)S(1)} %pad_maximum_fusion), channel_id=1, replica_groups=mesh['zlo'=8,'zhi'=4,'y'=4,'core'=2,'x'=4] {'x'}, dimensions={0}, use_global_device_ids=true | all-gather | bytes 450560 | tf_op jit(solution)/shard_map/all_gather | solution.py:274
  47.4 0.4 upstream_terms.1
  47.9 21.4 %all-to-all-done.x_ref = bf16[32,24,128]{2,1,0:T(8,128)(2,1)S(1)} async-done(((bf16[32,24,128]{2,1,0:T(8,128)(2,1)}), bf16[32,24,128]{2,1,0:T(8,128)(2,1)S(1)}, u32[]{:S(2)}, u32[]{:S(2)}) %all-to-all-start) | async-done | bytes 196640 | tf_op jit(solution)/shard_map/all_to_all | solution.py:263
  69.2 1.2 layer_terms.1
  70.5 17.9 %all_to_all.25.in_ref = bf16[32,80,128]{2,1,0:T(8,128)(2,1)S(1)} all-to-all(bf16[32,80,128]{2,1,0:T(8,128)(2,1)S(1)} %get-tuple-element.24), channel_id=1, replica_groups=mesh['zlo'=8,'zhi'=4,'y'=4,'core'=2,'x'=4] {'y','core','x'}, dimensions={0} | all-to-all | bytes 1310720 | tf_op jit(solution)/shard_map/all_to_all | solution.py:263
  88.4 0.8 plane_terms.1
  89.2 7.8 %all-to-all-start.2 = ((bf16[4,240,128]{2,1,0:T(8,128)(2,1)}), bf16[4,240,128]{2,1,0:T(8,128)(2,1)S(1)}, u32[]{:S(2)}, u32[]{:S(2)}) async-start(bf16[4,240,128]{2,1,0:T(8,128)(2,1)} %plane_terms.1), calls=%async_computation.2 | async-start | bytes 491520 | tf_op jit(solution)/shard_map/all_to_all | solution.py:263
  97.0 0.1 copy.18
  97.2 11.1 %all_gather.7 = bf16[8,256,192]{1,2,0:T(8,128)(2,1)S(1)} all-gather(bf16[2,256,192]{1,2,0:T(8,128)(2,1)S(1)} %copy.18), channel_id=1, replica_groups=mesh['zlo'=8,'zhi'=4,'y'=4,'core'=2,'x'=4] {'x'}, dimensions={0}, use_global_device_ids=true | all-gather | bytes 983040 | tf_op jit(solution)/shard_map/all_gather | solution.py:279
  108.2 18.0 %all-to-all-done.2.in_ref = bf16[4,240,128]{2,1,0:T(8,128)(2,1)S(1)} async-done(((bf16[4,240,128]{2,1,0:T(8,128)(2,1)}), bf16[4,240,128]{2,1,0:T(8,128)(2,1)S(1)}, u32[]{:S(2)}, u32[]{:S(2)}) %all-to-all-start.2) | async-done | bytes 245792 | tf_op jit(solution)/shard_map/all_to_all | solution.py:263
  126.2 0.3 column_terms.1
  126.5 22.4 %all_to_all.26.in_ref = bf16[8,48,128]{2,1,0:T(8,128)(2,1)S(1)} all-to-all(bf16[8,48,128]{2,1,0:T(8,128)(2,1)S(1)} %get-tuple-element.27), channel_id=1, replica_groups=mesh['zlo'=8,'zhi'=4,'y'=4,'core'=2,'x'=4] {'zlo'}, dimensions={0} | all-to-all | bytes 196608 | tf_op jit(solution)/shard_map/all_to_all | solution.py:263
  148.9 0.7 replica_terms.1
  149.6 7.1 %all-to-all-start.4 = ((f32[8,48,128]{2,1,0:T(8,128)}), f32[8,48,128]{2,1,0:T(8,128)S(1)}, u32[]{:S(2)}, u32[]{:S(2)}) async-start(f32[8,48,128]{2,1,0:T(8,128)} %replica_terms.1), calls=%async_computation.4 | async-start | bytes 393216 | tf_op jit(solution)/shard_map/all_to_all | solution.py:263
  156.7 1.0 copy.19
  157.7 4.9 %all-to-all-done.4.refs_0_ = f32[8,48,128]{2,1,0:T(8,128)S(1)} async-done(((f32[8,48,128]{2,1,0:T(8,128)}), f32[8,48,128]{2,1,0:T(8,128)S(1)}, u32[]{:S(2)}, u32[]{:S(2)}) %all-to-all-start.4) | async-done | bytes 196640 | tf_op jit(solution)/shard_map/all_to_all | solution.py:263
  162.6 0.7 final_terms.1
  163.3 0.9 copy.21
  (7 shorter events, 0.0 us)
Async XLA Ops:
  2.5 33.4 %copy-start = (bf16[8,256,192]{1,2,0:T(8,128)(2,1)S(1)}, bf16[8,256,192]{1,2,0:T(8,128)(2,1)}, u32[]{:S(2)}) copy-start(bf16[8,256,192]{1,2,0:T(8,128)(2,1)} %param.9) | copy-start | bytes 2359300
  3.2 66.0 %all-to-all-start = ((bf16[32,24,128]{2,1,0:T(8,128)(2,1)}), bf16[32,24,128]{2,1,0:T(8,128)(2,1)S(1)}, u32[]{:S(2)}, u32[]{:S(2)}) async-start(bf16[32,24,128]{2,1,0:T(8,128)(2,1)} %pack_rows.1), calls=%async_computation | async-start | bytes 393216 | tf_op jit(solution)/shard_map/all_to_all | solution.py:263
  35.9 0.8 copy-start.1
  35.9 0.8 copy-start.2
  35.9 0.8 copy-start.3
  89.2 37.0 %all-to-all-start.2 = ((bf16[4,240,128]{2,1,0:T(8,128)(2,1)}), bf16[4,240,128]{2,1,0:T(8,128)(2,1)S(1)}, u32[]{:S(2)}, u32[]{:S(2)}) async-start(bf16[4,240,128]{2,1,0:T(8,128)(2,1)} %plane_terms.1), calls=%async_computation.2 | async-start | bytes 491520 | tf_op jit(solution)/shard_map/all_to_all | solution.py:263
  149.6 13.0 %all-to-all-start.4 = ((f32[8,48,128]{2,1,0:T(8,128)}), f32[8,48,128]{2,1,0:T(8,128)S(1)}, u32[]{:S(2)}, u32[]{:S(2)}) async-start(f32[8,48,128]{2,1,0:T(8,128)} %replica_terms.1), calls=%async_computation.4 | async-start | bytes 393216 | tf_op jit(solution)/shard_map/all_to_all | solution.py:263

commit v3 on v2

--- a/solution.py
+++ b/solution.py
@@ -10,6 +10,8 @@
 TABLE = ("zhi", "y", "core")
 PLANE = ("y", "core", "x")
 COLUMN = ("y", "core")
+TURN = 16
+GROUP = [[(i + TURN) % 32 for i in range(32)]]
 VMEM_BYTES = 48 * 1024 * 1024
 
 
@@ -36,7 +38,9 @@
     n = first.shape[0]
     mixed = jnp.concatenate([first[:, :, 128:], second[:, :, 128:]], axis=2)
     rows = jnp.concatenate([first[:, :, :128], second[:, :, :128], mixed], axis=1)
-    out_ref[...] = rows.astype(BF).reshape(n, 24, 128)
+    rows = rows.astype(BF)
+    out_ref[0 : n - TURN] = rows[TURN:]
+    out_ref[n - TURN :] = rows[:TURN]
 
 
 def pack_rows(t, pooled):
@@ -103,6 +107,7 @@
     out_w = w_ref[:, 512:704]
     wt = wt_ref[...]
     planes = x_ref[...].astype(F32)
+    planes = jnp.concatenate([planes[32 - TURN :], planes[: 32 - TURN]], axis=0)
     plane = [planes[:, 8 * i : 8 * i + 8].reshape(256, 128) for i in range(3)]
     xs = [
         jnp.concatenate([plane[0], plane[2][:, :64]], axis=1),
@@ -168,11 +173,25 @@
     )(t, rows, cotangent, weights, ig, igt, base, wt, p)
 
 
-def plane_kernel(in_ref, out_ref):
+def weight_kernel(in_ref, out_ref):
     total = in_ref[0, 32:80].astype(F32)
     for d in range(1, 32):
         total = total + in_ref[d, 32:80].astype(F32)
     total = total.astype(BF)
+    for r in range(out_ref.shape[0]):
+        out_ref[r] = total
+
+
+def weight_terms(received, rep_count):
+    return pl.pallas_call(
+        weight_kernel,
+        out_shape=jax.ShapeDtypeStruct((rep_count, 48, 128), BF),
+        compiler_params=params(),
+        name="weight_terms",
+    )(received)
+
+
+def plane_kernel(in_ref, out_ref):
     wide = []
     for c in range(8):
         parts = [in_ref[4 * c + q, 0:32].astype(F32)[:, :96] for q in range(4)]
@@ -181,24 +200,42 @@
         rows = jnp.concatenate([wide[c][8 * z : 8 * z + 8] for c in range(8)], axis=0).astype(BF)
         for i in range(3):
             out_ref[z, 64 * i : 64 * i + 64] = rows[:, 128 * i : 128 * i + 128]
-        out_ref[z, 192:240] = total
 
 
 def plane_terms(received):
     return pl.pallas_call(
         plane_kernel,
-        out_shape=jax.ShapeDtypeStruct((4, 240, 128), BF),
+        out_shape=jax.ShapeDtypeStruct((4, 192, 128), BF),
         compiler_params=params(),
         name="plane_terms",
     )(received)
+
+
+def replica_kernel(weight_ref, emb_ref, out_ref):
+    total = weight_ref[0].astype(F32)
+    for r in range(1, weight_ref.shape[0]):
+        total = total + weight_ref[r].astype(F32)
+    total = total.astype(BF)
+    for z in range(4):
+        out_ref[z, 0:192] = emb_ref[z]
+        out_ref[z, 192:240] = total
+
+
+def replica_terms(weight, emb):
+    return pl.pallas_call(
+        replica_kernel,
+        out_shape=jax.ShapeDtypeStruct((4, 240, 128), BF),
+        compiler_params=params(),
+        name="replica_terms",
+    )(weight, emb)
 
 
 def column_kernel(in_ref, emb_ref, total_ref):
     total = in_ref[0, 192:240].astype(F32)
     for z in range(1, 4):
         total = total + in_ref[z, 192:240].astype(F32)
-    for r in range(total_ref.shape[0]):
-        total_ref[r] = total.astype(BF)
+    for c in range(8):
+        total_ref[c] = total
     for z in range(4):
         planes = [in_ref[z, 64 * i : 64 * i + 64].astype(F32) for i in range(3)]
         rows = jnp.concatenate(planes, axis=1).reshape(8, 8, 384)
@@ -206,33 +243,29 @@
             emb_ref[8 * z : 8 * z + 8, i] = rows[:, :, 48 * i : 48 * i + 48].astype(BF)
 
 
-def column_terms(received, rep_count):
+def column_terms(received):
     return pl.pallas_call(
         column_kernel,
         out_shape=[
             jax.ShapeDtypeStruct((32, 8, 8, 48), BF),
-            jax.ShapeDtypeStruct((rep_count, 48, 128), BF),
+            jax.ShapeDtypeStruct((8, 48, 128), F32),
         ],
         compiler_params=params(),
         name="column_terms",
     )(received)
 
 
-def replica_kernel(in_ref, out_ref):
-    total = in_ref[0].astype(F32)
-    for r in range(1, in_ref.shape[0]):
-        total = total + in_ref[r].astype(F32)
-    for c in range(8):
-        out_ref[c] = total
-
-
-def replica_terms(received):
-    return pl.pallas_call(
-        replica_kernel,
-        out_shape=jax.ShapeDtypeStruct((8, 48, 128), F32),
-        compiler_params=params(),
-        name="replica_terms",
-    )(received)
+def copy_kernel(in_ref, out_ref):
+    out_ref[...] = in_ref[...]
+
+
+def settle(block):
+    return pl.pallas_call(
+        copy_kernel,
+        out_shape=jax.ShapeDtypeStruct(block.shape, block.dtype),
+        compiler_params=params(),
+        name="settle",
+    )(block)
 
 
 def final_kernel(wide_scale, out_scale, in_ref, lc_ref, proj_ref, out_ref):
@@ -269,19 +302,21 @@
     sample_total = cotangent.shape[0] * rep_count * 32
     wide_scale = float(sample_total * 192) ** (-0.5)
     out_scale = float(sample_total * 256 * 192) ** (-0.5)
-    rows = swap(pack_rows(t, pooled), TABLE)
+    rows = lax.all_to_all(
+        pack_rows(t, pooled), TABLE, split_axis=0, concat_axis=0, tiled=True, axis_index_groups=GROUP
+    )
     own = jnp.concatenate([lc_weight, fm_proj.T, fm_out], axis=1)
     weights = lax.all_gather(own, "x", axis=0, tiled=True)
     ig, igt, base, wt, p = upstream_terms(t, cotangent, weights)
     layer, messages = layer_terms(t, rows, cotangent, weights, ig, igt, base, wt, p)
-    plane = plane_terms(swap(messages, PLANE))
-    column = swap(plane, "zhi")
-    layer_out = lax.all_gather(layer, "x", axis=0, tiled=True)
+    received = swap(messages, PLANE)
+    weight = swap(weight_terms(received, rep_count), "zlo")
+    column = swap(replica_terms(weight, plane_terms(received)), "zhi")
+    layer_out = settle(lax.all_gather(layer.transpose(0, 2, 1), "x", axis=0, tiled=True))
     column, _ = lax.optimization_barrier((column, layer_out))
-    emb_grad, total = column_terms(column, rep_count)
-    total = replica_terms(swap(total, "zlo"))
+    emb_grad, total = column_terms(column)
     lc_grad, proj_grad, out_grad = final_terms(swap(total, COLUMN), wide_scale, out_scale)
-    return (layer_out, emb_grad.reshape(256, 8, 48), lc_grad, proj_grad.T, out_grad)
+    return (layer_out.transpose(0, 2, 1), emb_grad.reshape(256, 8, 48), lc_grad, proj_grad.T, out_grad)
 
 
 def solution(mesh):

time: 165 us -> 166 us (level)
  the two profiles are of different devices: /device:TPU:1 before, /device:TPU:34 now
where the time goes in v3:
time: 166 us; the launch traced here: 165 us
  starting transfers between devices  64.7 us (39%)
  waiting for transfers between devices  46.4 us (28%)
  blocking collectives  43.2 us (26%)
  Pallas kernels  6.49 us (4%)
  local copies, waits for them, and re-layouts  3.72 us (2%)
    all_to_all x3, waiting for transfers between devices, swap(): return lax.all_to_all(blocks, axes, split_axis=0, concat_axis=0, tiled=True)  40.3 us
    all_to_all x1, starting transfers between devices, shards(): lax.all_to_all(pack_rows(t, pooled), TABLE, split_axis=0, concat_axis=0,...  34.4 us
    all_to_all x3, starting transfers between devices, swap(): return lax.all_to_all(blocks, axes, split_axis=0, concat_axis=0, tiled=True)  30.3 us
    all_to_all x1, blocking collectives, swap(): return lax.all_to_all(blocks, axes, split_axis=0, concat_axis=0, tiled=True)  16.1 us
    all_gather x1, blocking collectives, shards(): lax.all_gather(layer.transpose(0, 2, 1), 'x', axis=0, tiled=True)  14.5 us
    all_gather x1, blocking collectives, shards(): weights = lax.all_gather(own, 'x', axis=0, tiled=True)  12.6 us
    all_to_all x1, waiting for transfers between devices, shards(): lax.all_to_all(pack_rows(t, pooled), TABLE, split_axis=0, concat_axis=0,...  6.15 us
    unnamed x11, local copies, waits for them, and re-layouts  3.58 us
  transfers between devices with their start and end apart: 4, of which 4 were waited for; matrix products, arithmetic and copies ran while one was open for 1% of the time, Pallas kernels for 1%

profile of v3, /device:TPU:34, one launch (start us, length us, event | category | flops | bytes accessed | tf_op | source)
XLA Modules:
  0.0 165.3 jit_solution(14335512741900252478)
XLA Ops:
  0.6 1.8 %copy.15 = bf16[256,8,192]{2,1,0:T(8,128)(2,1)S(1)} copy(bf16[256,8,192]{0,2,1:T(8,128)(2,1)} %param.5) | data formatting | bytes 1572864 | tf_op args[0]
  2.5 0.8 pack_rows.1
  3.2 34.4 %all-to-all-start = ((bf16[32,24,128]{2,1,0:T(8,128)(2,1)}), bf16[32,24,128]{2,1,0:T(8,128)(2,1)S(1)}, u32[]{:S(2)}, u32[]{:S(2)}) async-start(bf16[32,24,128]{2,1,0:T(8,128)(2,1)} %pack_rows.1), calls=%async_computation | async-start | bytes 393216 | tf_op jit(solution)/shard_map/all_to_all | solution.py:305
  37.7 0.5 copy.17.g_ref
  38.2 0.2 copy-done.1
  38.5 12.6 %all_gather.6.w_ref = bf16[256,704]{1,0:T(8,128)(2,1)S(1)} all-gather(bf16[64,704]{1,0:T(8,128)(2,1)S(1)} %pad_maximum_fusion), channel_id=1, replica_groups=mesh['zlo'=8,'zhi'=4,'y'=4,'core'=2,'x'=4] {'x'}, dimensions={0}, use_global_device_ids=true | all-gather | bytes 450560 | tf_op jit(solution)/shard_map/all_gather | solution.py:309
  51.1 0.4 upstream_terms.1
  51.5 6.1 %all-to-all-done.x_ref = bf16[32,24,128]{2,1,0:T(8,128)(2,1)S(1)} async-done(((bf16[32,24,128]{2,1,0:T(8,128)(2,1)}), bf16[32,24,128]{2,1,0:T(8,128)(2,1)S(1)}, u32[]{:S(2)}, u32[]{:S(2)}) %all-to-all-start) | async-done | bytes 196640 | tf_op jit(solution)/shard_map/all_to_all | solution.py:305
  57.6 1.2 layer_terms.1
  58.9 16.1 %all_to_all.25.in_ref = bf16[32,80,128]{2,1,0:T(8,128)(2,1)S(1)} all-to-all(bf16[32,80,128]{2,1,0:T(8,128)(2,1)S(1)} %get-tuple-element.24), channel_id=1, replica_groups=mesh['zlo'=8,'zhi'=4,'y'=4,'core'=2,'x'=4] {'y','core','x'}, dimensions={0} | all-to-all | bytes 1310720 | tf_op jit(solution)/shard_map/all_to_all | solution.py:296
  75.0 0.7 weight_terms.1
  75.7 5.9 %all-to-all-start.2 = ((bf16[8,48,128]{2,1,0:T(8,128)(2,1)}), bf16[8,48,128]{2,1,0:T(8,128)(2,1)S(1)}, u32[]{:S(2)}, u32[]{:S(2)}) async-start(bf16[8,48,128]{2,1,0:T(8,128)(2,1)} %weight_terms.1), calls=%async_computation.2 | async-start | bytes 196608 | tf_op jit(solution)/shard_map/all_to_all | solution.py:296
  81.7 9.8 %all-to-all-done.2.weight_ref = bf16[8,48,128]{2,1,0:T(8,128)(2,1)S(1)} async-done(((bf16[8,48,128]{2,1,0:T(8,128)(2,1)}), bf16[8,48,128]{2,1,0:T(8,128)(2,1)S(1)}, u32[]{:S(2)}, u32[]{:S(2)}) %all-to-all-start.2) | async-done | bytes 98336 | tf_op jit(solution)/shard_map/all_to_all | solution.py:296
  91.5 0.7 replica_terms.1
  92.3 20.8 %all-to-all-start.3 = ((bf16[4,240,128]{2,1,0:T(8,128)(2,1)}), bf16[4,240,128]{2,1,0:T(8,128)(2,1)S(1)}, u32[]{:S(2)}, u32[]{:S(2)}) async-start(bf16[4,240,128]{2,1,0:T(8,128)(2,1)} %replica_terms.1), calls=%async_computation.3 | async-start | bytes 491520 | tf_op jit(solution)/shard_map/all_to_all | solution.py:296
  113.1 0.1 copy.18
  113.2 14.5 %all_gather.7.in_ref = bf16[8,192,256]{2,1,0:T(8,128)(2,1)S(1)} all-gather(bf16[2,192,256]{2,1,0:T(8,128)(2,1)S(1)} %copy.18), channel_id=1, replica_groups=mesh['zlo'=8,'zhi'=4,'y'=4,'core'=2,'x'=4] {'x'}, dimensions={0}, use_global_device_ids=true | all-gather | bytes 983040 | tf_op jit(solution)/shard_map/all_gather | solution.py:315
  127.7 0.9 settle.1
  128.6 24.6 %all-to-all-done.3.in_ref = bf16[4,240,128]{2,1,0:T(8,128)(2,1)S(1)} async-done(((bf16[4,240,128]{2,1,0:T(8,128)(2,1)}), bf16[4,240,128]{2,1,0:T(8,128)(2,1)S(1)}, u32[]{:S(2)}, u32[]{:S(2)}) %all-to-all-start.3) | async-done | bytes 245792 | tf_op jit(solution)/shard_map/all_to_all | solution.py:296
  153.2 0.9 column_terms.1
  154.1 3.6 %all-to-all-start.4 = ((f32[8,48,128]{2,1,0:T(8,128)}), f32[8,48,128]{2,1,0:T(8,128)S(1)}, u32[]{:S(2)}, u32[]{:S(2)}) async-start(f32[8,48,128]{2,1,0:T(8,128)} %get-tuple-element.27), calls=%async_computation.4 | async-start | bytes 393216 | tf_op jit(solution)/shard_map/all_to_all | solution.py:296
  157.8 1.0 copy.19
  158.8 5.8 %all-to-all-done.4.refs_0_ = f32[8,48,128]{2,1,0:T(8,128)S(1)} async-done(((f32[8,48,128]{2,1,0:T(8,128)}), f32[8,48,128]{2,1,0:T(8,128)S(1)}, u32[]{:S(2)}, u32[]{:S(2)}) %all-to-all-start.4) | async-done | bytes 196640 | tf_op jit(solution)/shard_map/all_to_all | solution.py:296
  164.6 0.7 final_terms.1
  (9 shorter events, 0.2 us)
Async XLA Ops:
  2.5 35.2 %copy-start = (bf16[8,256,192]{1,2,0:T(8,128)(2,1)S(1)}, bf16[8,256,192]{1,2,0:T(8,128)(2,1)}, u32[]{:S(2)}) copy-start(bf16[8,256,192]{1,2,0:T(8,128)(2,1)} %param.9) | copy-start | bytes 2359300
  3.2 54.4 %all-to-all-start = ((bf16[32,24,128]{2,1,0:T(8,128)(2,1)}), bf16[32,24,128]{2,1,0:T(8,128)(2,1)S(1)}, u32[]{:S(2)}, u32[]{:S(2)}) async-start(bf16[32,24,128]{2,1,0:T(8,128)(2,1)} %pack_rows.1), calls=%async_computation | async-start | bytes 393216 | tf_op jit(solution)/shard_map/all_to_all | solution.py:305
  37.7 0.8 copy-start.1
  37.7 0.8 copy-start.2
  37.7 0.8 copy-start.3
  75.7 15.8 %all-to-all-start.2 = ((bf16[8,48,128]{2,1,0:T(8,128)(2,1)}), bf16[8,48,128]{2,1,0:T(8,128)(2,1)S(1)}, u32[]{:S(2)}, u32[]{:S(2)}) async-start(bf16[8,48,128]{2,1,0:T(8,128)(2,1)} %weight_terms.1), calls=%async_computation.2 | async-start | bytes 196608 | tf_op jit(solution)/shard_map/all_to_all | solution.py:296
  92.3 61.0 %all-to-all-start.3 = ((bf16[4,240,128]{2,1,0:T(8,128)(2,1)}), bf16[4,240,128]{2,1,0:T(8,128)(2,1)S(1)}, u32[]{:S(2)}, u32[]{:S(2)}) async-start(bf16[4,240,128]{2,1,0:T(8,128)(2,1)} %replica_terms.1), calls=%async_computation.3 | async-start | bytes 491520 | tf_op jit(solution)/shard_map/all_to_all | solution.py:296
  154.1 10.5 %all-to-all-start.4 = ((f32[8,48,128]{2,1,0:T(8,128)}), f32[8,48,128]{2,1,0:T(8,128)S(1)}, u32[]{:S(2)}, u32[]{:S(2)}) async-start(f32[8,48,128]{2,1,0:T(8,128)} %get-tuple-element.27), calls=%async_computation.4 | async-start | bytes 393216 | tf_op jit(solution)/shard_map/all_to_all | solution.py:296

commit v4 on v3

--- a/solution.py
+++ b/solution.py
@@ -11,7 +11,8 @@
 PLANE = ("y", "core", "x")
 COLUMN = ("y", "core")
 TURN = 16
-GROUP = [[(i + TURN) % 32 for i in range(32)]]
+TABLE_ORDER = [(i + TURN) % 32 for i in range(32)]
+COLUMN_ORDER = [2, 3, 0, 1]
 VMEM_BYTES = 48 * 1024 * 1024
 
 
@@ -217,7 +218,7 @@
         total = total + weight_ref[r].astype(F32)
     total = total.astype(BF)
     for z in range(4):
-        out_ref[z, 0:192] = emb_ref[z]
+        out_ref[(z + 2) % 4, 0:192] = emb_ref[z]
         out_ref[z, 192:240] = total
 
 
@@ -230,14 +231,27 @@
     )(weight, emb)
 
 
-def column_kernel(in_ref, emb_ref, total_ref):
+def total_kernel(in_ref, out_ref):
     total = in_ref[0, 192:240].astype(F32)
     for z in range(1, 4):
         total = total + in_ref[z, 192:240].astype(F32)
+    total = total.astype(BF)
     for c in range(8):
-        total_ref[c] = total
+        out_ref[c] = total
+
+
+def total_terms(received):
+    return pl.pallas_call(
+        total_kernel,
+        out_shape=jax.ShapeDtypeStruct((8, 48, 128), BF),
+        compiler_params=params(),
+        name="total_terms",
+    )(received)
+
+
+def column_kernel(in_ref, emb_ref):
     for z in range(4):
-        planes = [in_ref[z, 64 * i : 64 * i + 64].astype(F32) for i in range(3)]
+        planes = [in_ref[(z + 2) % 4, 64 * i : 64 * i + 64].astype(F32) for i in range(3)]
         rows = jnp.concatenate(planes, axis=1).reshape(8, 8, 384)
         for i in range(8):
             emb_ref[8 * z : 8 * z + 8, i] = rows[:, :, 48 * i : 48 * i + 48].astype(BF)
@@ -246,10 +260,7 @@
 def column_terms(received):
     return pl.pallas_call(
         column_kernel,
-        out_shape=[
-            jax.ShapeDtypeStruct((32, 8, 8, 48), BF),
-            jax.ShapeDtypeStruct((8, 48, 128), F32),
-        ],
+        out_shape=jax.ShapeDtypeStruct((32, 8, 8, 48), BF),
         compiler_params=params(),
         name="column_terms",
     )(received)
@@ -269,7 +280,7 @@
 
 
 def final_kernel(wide_scale, out_scale, in_ref, lc_ref, proj_ref, out_ref):
-    rows = [in_ref[c] for c in range(8)]
+    rows = [in_ref[c].astype(F32) for c in range(8)]
     part = [jnp.concatenate([r[8 * i : 8 * i + 8] for r in rows], axis=0) for i in range(6)]
     lc_ref[...] = jnp.concatenate(part[0:2], axis=1) * wide_scale
     proj_ref[...] = jnp.concatenate(part[2:4], axis=1) * wide_scale
@@ -292,8 +303,9 @@
     )(received)
 
 
-def swap(blocks, axes):
-    return lax.all_to_all(blocks, axes, split_axis=0, concat_axis=0, tiled=True)
+def swap(blocks, axes, order=None):
+    groups = None if order is None else [order]
+    return lax.all_to_all(blocks, axes, split_axis=0, concat_axis=0, tiled=True, axis_index_groups=groups)
 
 
 def shards(pooled, lc_weight, fm_proj, fm_out, cotangent):
@@ -302,20 +314,20 @@
     sample_total = cotangent.shape[0] * rep_count * 32
     wide_scale = float(sample_total * 192) ** (-0.5)
     out_scale = float(sample_total * 256 * 192) ** (-0.5)
-    rows = lax.all_to_all(
-        pack_rows(t, pooled), TABLE, split_axis=0, concat_axis=0, tiled=True, axis_index_groups=GROUP
-    )
+    middle_first = sorted(range(rep_count), key=lambda r: abs(2 * r - rep_count))
+    rows = swap(pack_rows(t, pooled), TABLE, TABLE_ORDER)
     own = jnp.concatenate([lc_weight, fm_proj.T, fm_out], axis=1)
     weights = lax.all_gather(own, "x", axis=0, tiled=True)
     ig, igt, base, wt, p = upstream_terms(t, cotangent, weights)
     layer, messages = layer_terms(t, rows, cotangent, weights, ig, igt, base, wt, p)
     received = swap(messages, PLANE)
-    weight = swap(weight_terms(received, rep_count), "zlo")
-    column = swap(replica_terms(weight, plane_terms(received)), "zhi")
+    weight = swap(weight_terms(received, rep_count), "zlo", middle_first)
+    column = swap(replica_terms(weight, plane_terms(received)), "zhi", COLUMN_ORDER)
     layer_out = settle(lax.all_gather(layer.transpose(0, 2, 1), "x", axis=0, tiled=True))
     column, _ = lax.optimization_barrier((column, layer_out))
-    emb_grad, total = column_terms(column)
-    lc_grad, proj_grad, out_grad = final_terms(swap(total, COLUMN), wide_scale, out_scale)
+    total = swap(total_terms(column), COLUMN)
+    emb_grad = column_terms(column)
+    lc_grad, proj_grad, out_grad = final_terms(total, wide_scale, out_scale)
     return (layer_out.transpose(0, 2, 1), emb_grad.reshape(256, 8, 48), lc_grad, proj_grad.T, out_grad)
 
 

time: 166 us -> 147 us (0.89)
  the two profiles are of different devices: /device:TPU:34 before, /device:TPU:1 now
where the time goes in v4:
time: 147 us; the launch traced here: 146 us
  starting transfers between devices  72 us (49%)
  blocking collectives  40.8 us (28%)
  waiting for transfers between devices  22.5 us (15%)
  Pallas kernels  6.49 us (4%)
  local copies, waits for them, and re-layouts  3.72 us (3%)
    all_to_all x4, starting transfers between devices, swap(): lax.all_to_all(blocks, axes, split_axis=0, concat_axis=0, tiled=True, axi...  72 us
    all_to_all x4, waiting for transfers between devices, swap(): lax.all_to_all(blocks, axes, split_axis=0, concat_axis=0, tiled=True, axi...  22.5 us
    all_to_all x1, blocking collectives, swap(): lax.all_to_all(blocks, axes, split_axis=0, concat_axis=0, tiled=True, axi...  17.5 us
    all_gather x1, blocking collectives, shards(): lax.all_gather(layer.transpose(0, 2, 1), 'x', axis=0, tiled=True)  12.5 us
    all_gather x1, blocking collectives, shards(): weights = lax.all_gather(own, 'x', axis=0, tiled=True)  10.9 us
    unnamed x11, local copies, waits for them, and re-layouts  3.59 us
  transfers between devices with their start and end apart: 4, of which 4 were waited for; matrix products, arithmetic and copies ran while one was open for 1% of the time, Pallas kernels for 1%

profile of v4, /device:TPU:1, one launch (start us, length us, event | category | flops | bytes accessed | tf_op | source)
XLA Modules:
  0.0 146.2 jit_solution(16410076209346761600)
XLA Ops:
  0.6 1.8 %copy.15 = bf16[256,8,192]{2,1,0:T(8,128)(2,1)S(1)} copy(bf16[256,8,192]{0,2,1:T(8,128)(2,1)} %param.5) | data formatting | bytes 1572864 | tf_op args[0]
  2.5 0.8 pack_rows.1
  3.2 36.5 %all-to-all-start = ((bf16[32,24,128]{2,1,0:T(8,128)(2,1)}), bf16[32,24,128]{2,1,0:T(8,128)(2,1)S(1)}, u32[]{:S(2)}, u32[]{:S(2)}) async-start(bf16[32,24,128]{2,1,0:T(8,128)(2,1)} %pack_rows.1), calls=%async_computation | async-start | bytes 393216 | tf_op jit(solution)/shard_map/all_to_all | solution.py:308
  39.8 0.5 copy.17.g_ref
  40.3 0.2 copy-done.1
  40.5 10.9 %all_gather.6.w_ref = bf16[256,704]{1,0:T(8,128)(2,1)S(1)} all-gather(bf16[64,704]{1,0:T(8,128)(2,1)S(1)} %pad_maximum_fusion), channel_id=1, replica_groups=mesh['zlo'=8,'zhi'=4,'y'=4,'core'=2,'x'=4] {'x'}, dimensions={0}, use_global_device_ids=true | all-gather | bytes 450560 | tf_op jit(solution)/shard_map/all_gather | solution.py:320
  51.4 0.4 upstream_terms.1
  51.8 8.5 %all-to-all-done.x_ref = bf16[32,24,128]{2,1,0:T(8,128)(2,1)S(1)} async-done(((bf16[32,24,128]{2,1,0:T(8,128)(2,1)}), bf16[32,24,128]{2,1,0:T(8,128)(2,1)S(1)}, u32[]{:S(2)}, u32[]{:S(2)}) %all-to-all-start) | async-done | bytes 196640 | tf_op jit(solution)/shard_map/all_to_all | solution.py:308
  60.4 1.2 layer_terms.1
  61.6 17.5 %all_to_all.25.in_ref = bf16[32,80,128]{2,1,0:T(8,128)(2,1)S(1)} all-to-all(bf16[32,80,128]{2,1,0:T(8,128)(2,1)S(1)} %get-tuple-element.22), channel_id=1, replica_groups=mesh['zlo'=8,'zhi'=4,'y'=4,'core'=2,'x'=4] {'y','core','x'}, dimensions={0} | all-to-all | bytes 1310720 | tf_op jit(solution)/shard_map/all_to_all | solution.py:308
  79.1 0.7 weight_terms.1
  79.8 6.6 %all-to-all-start.2 = ((bf16[8,48,128]{2,1,0:T(8,128)(2,1)}), bf16[8,48,128]{2,1,0:T(8,128)(2,1)S(1)}, u32[]{:S(2)}, u32[]{:S(2)}) async-start(bf16[8,48,128]{2,1,0:T(8,128)(2,1)} %weight_terms.1), calls=%async_computation.2 | async-start | bytes 196608 | tf_op jit(solution)/shard_map/all_to_all | solution.py:308
  86.5 4.8 %all-to-all-done.2.weight_ref = bf16[8,48,128]{2,1,0:T(8,128)(2,1)S(1)} async-done(((bf16[8,48,128]{2,1,0:T(8,128)(2,1)}), bf16[8,48,128]{2,1,0:T(8,128)(2,1)S(1)}, u32[]{:S(2)}, u32[]{:S(2)}) %all-to-all-start.2) | async-done | bytes 98336 | tf_op jit(solution)/shard_map/all_to_all | solution.py:308
  91.4 0.7 replica_terms.1
  92.1 22.0 %all-to-all-start.3 = ((bf16[4,240,128]{2,1,0:T(8,128)(2,1)}), bf16[4,240,128]{2,1,0:T(8,128)(2,1)S(1)}, u32[]{:S(2)}, u32[]{:S(2)}) async-start(bf16[4,240,128]{2,1,0:T(8,128)(2,1)} %replica_terms.1), calls=%async_computation.3 | async-start | bytes 491520 | tf_op jit(solution)/shard_map/all_to_all | solution.py:308
  114.3 12.5 %all_gather.7.in_ref = bf16[8,192,256]{2,1,0:T(8,128)(2,1)S(1)} all-gather(bf16[2,192,256]{2,1,0:T(8,128)(2,1)S(1)} %copy.18), channel_id=1, replica_groups=mesh['zlo'=8,'zhi'=4,'y'=4,'core'=2,'x'=4] {'x'}, dimensions={0}, use_global_device_ids=true | all-gather | bytes 983040 | tf_op jit(solution)/shard_map/all_gather | solution.py:326
  126.7 0.9 settle.1
  127.7 5.4 %all-to-all-done.3.in_ref = bf16[4,240,128]{2,1,0:T(8,128)(2,1)S(1)} async-done(((bf16[4,240,128]{2,1,0:T(8,128)(2,1)}), bf16[4,240,128]{2,1,0:T(8,128)(2,1)S(1)}, u32[]{:S(2)}, u32[]{:S(2)}) %all-to-all-start.3) | async-done | bytes 245792 | tf_op jit(solution)/shard_map/all_to_all | solution.py:308
  133.1 0.6 total_terms.1
  133.8 6.8 %all-to-all-start.4 = ((bf16[8,48,128]{2,1,0:T(8,128)(2,1)}), bf16[8,48,128]{2,1,0:T(8,128)(2,1)S(1)}, u32[]{:S(2)}, u32[]{:S(2)}) async-start(bf16[8,48,128]{2,1,0:T(8,128)(2,1)} %total_terms.1), calls=%async_computation.4 | async-start | bytes 196608 | tf_op jit(solution)/shard_map/all_to_all | solution.py:308
  140.6 0.3 column_terms.1
  140.9 1.0 copy.19
  141.9 3.7 %all-to-all-done.4.refs_0_ = bf16[8,48,128]{2,1,0:T(8,128)(2,1)S(1)} async-done(((bf16[8,48,128]{2,1,0:T(8,128)(2,1)}), bf16[8,48,128]{2,1,0:T(8,128)(2,1)S(1)}, u32[]{:S(2)}, u32[]{:S(2)}) %all-to-all-start.4) | async-done | bytes 98336 | tf_op jit(solution)/shard_map/all_to_all | solution.py:308
  145.6 0.7 final_terms.1
  (10 shorter events, 0.3 us)
Async XLA Ops:
  2.5 37.3 %copy-start = (bf16[8,256,192]{1,2,0:T(8,128)(2,1)S(1)}, bf16[8,256,192]{1,2,0:T(8,128)(2,1)}, u32[]{:S(2)}) copy-start(bf16[8,256,192]{1,2,0:T(8,128)(2,1)} %param.9) | copy-start | bytes 2359300
  3.2 57.1 %all-to-all-start = ((bf16[32,24,128]{2,1,0:T(8,128)(2,1)}), bf16[32,24,128]{2,1,0:T(8,128)(2,1)S(1)}, u32[]{:S(2)}, u32[]{:S(2)}) async-start(bf16[32,24,128]{2,1,0:T(8,128)(2,1)} %pack_rows.1), calls=%async_computation | async-start | bytes 393216 | tf_op jit(solution)/shard_map/all_to_all | solution.py:308
  39.7 0.8 copy-start.1
  39.7 0.8 copy-start.2
  39.8 0.8 copy-start.3
  79.8 11.6 %all-to-all-start.2 = ((bf16[8,48,128]{2,1,0:T(8,128)(2,1)}), bf16[8,48,128]{2,1,0:T(8,128)(2,1)S(1)}, u32[]{:S(2)}, u32[]{:S(2)}) async-start(bf16[8,48,128]{2,1,0:T(8,128)(2,1)} %weight_terms.1), calls=%async_computation.2 | async-start | bytes 196608 | tf_op jit(solution)/shard_map/all_to_all | solution.py:308
  92.1 41.1 %all-to-all-start.3 = ((bf16[4,240,128]{2,1,0:T(8,128)(2,1)}), bf16[4,240,128]{2,1,0:T(8,128)(2,1)S(1)}, u32[]{:S(2)}, u32[]{:S(2)}) async-start(bf16[4,240,128]{2,1,0:T(8,128)(2,1)} %replica_terms.1), calls=%async_computation.3 | async-start | bytes 491520 | tf_op jit(solution)/shard_map/all_to_all | solution.py:308
  133.8 11.8 %all-to-all-start.4 = ((bf16[8,48,128]{2,1,0:T(8,128)(2,1)}), bf16[8,48,128]{2,1,0:T(8,128)(2,1)S(1)}, u32[]{:S(2)}, u32[]{:S(2)}) async-start(bf16[8,48,128]{2,1,0:T(8,128)(2,1)} %total_terms.1), calls=%async_computation.4 | async-start | bytes 196608 | tf_op jit(solution)/shard_map/all_to_all | solution.py:308

commit v5 on v4

--- a/solution.py
+++ b/solution.py
@@ -10,9 +10,9 @@
 TABLE = ("zhi", "y", "core")
 PLANE = ("y", "core", "x")
 COLUMN = ("y", "core")
-TURN = 16
-TABLE_ORDER = [(i + TURN) % 32 for i in range(32)]
 COLUMN_ORDER = [2, 3, 0, 1]
+FAR_FIRST = [5, 4, 7, 6, 1, 0, 3, 2]
+TABLE_ORDER = [8 * z + c for z in COLUMN_ORDER for c in FAR_FIRST]
 VMEM_BYTES = 48 * 1024 * 1024
 
 
@@ -36,12 +36,11 @@
 def pack_kernel(t_ref, pooled_ref, out_ref):
     first = pooled_ref[:, 0, 0].astype(F32)
     second = pooled_ref[:, 0, 1].astype(F32)
-    n = first.shape[0]
     mixed = jnp.concatenate([first[:, :, 128:], second[:, :, 128:]], axis=2)
     rows = jnp.concatenate([first[:, :, :128], second[:, :, :128], mixed], axis=1)
     rows = rows.astype(BF)
-    out_ref[0 : n - TURN] = rows[TURN:]
-    out_ref[n - TURN :] = rows[:TURN]
+    for k, d in enumerate(TABLE_ORDER):
+        out_ref[k] = rows[d]
 
 
 def pack_rows(t, pooled):
@@ -108,7 +107,7 @@
     out_w = w_ref[:, 512:704]
     wt = wt_ref[...]
     planes = x_ref[...].astype(F32)
-    planes = jnp.concatenate([planes[32 - TURN :], planes[: 32 - TURN]], axis=0)
+    planes = jnp.stack([planes[TABLE_ORDER.index(d)] for d in range(32)], axis=0)
     plane = [planes[:, 8 * i : 8 * i + 8].reshape(256, 128) for i in range(3)]
     xs = [
         jnp.concatenate([plane[0], plane[2][:, :64]], axis=1),
@@ -218,7 +217,7 @@
         total = total + weight_ref[r].astype(F32)
     total = total.astype(BF)
     for z in range(4):
-        out_ref[(z + 2) % 4, 0:192] = emb_ref[z]
+        out_ref[COLUMN_ORDER.index(z), 0:192] = emb_ref[z]
         out_ref[z, 192:240] = total
 
 
@@ -251,7 +250,7 @@
 
 def column_kernel(in_ref, emb_ref):
     for z in range(4):
-        planes = [in_ref[(z + 2) % 4, 64 * i : 64 * i + 64].astype(F32) for i in range(3)]
+        planes = [in_ref[COLUMN_ORDER.index(z), 64 * i : 64 * i + 64].astype(F32) for i in range(3)]
         rows = jnp.concatenate(planes, axis=1).reshape(8, 8, 384)
         for i in range(8):
             emb_ref[8 * z : 8 * z + 8, i] = rows[:, :, 48 * i : 48 * i + 48].astype(BF)
@@ -280,7 +279,7 @@
 
 
 def final_kernel(wide_scale, out_scale, in_ref, lc_ref, proj_ref, out_ref):
-    rows = [in_ref[c].astype(F32) for c in range(8)]
+    rows = [in_ref[FAR_FIRST.index(c)].astype(F32) for c in range(8)]
     part = [jnp.concatenate([r[8 * i : 8 * i + 8] for r in rows], axis=0) for i in range(6)]
     lc_ref[...] = jnp.concatenate(part[0:2], axis=1) * wide_scale
     proj_ref[...] = jnp.concatenate(part[2:4], axis=1) * wide_scale
@@ -325,7 +324,7 @@
     column = swap(replica_terms(weight, plane_terms(received)), "zhi", COLUMN_ORDER)
     layer_out = settle(lax.all_gather(layer.transpose(0, 2, 1), "x", axis=0, tiled=True))
     column, _ = lax.optimization_barrier((column, layer_out))
-    total = swap(total_terms(column), COLUMN)
+    total = swap(total_terms(column), COLUMN, FAR_FIRST)
     emb_grad = column_terms(column)
     lc_grad, proj_grad, out_grad = final_terms(total, wide_scale, out_scale)
     return (layer_out.transpose(0, 2, 1), emb_grad.reshape(256, 8, 48), lc_grad, proj_grad.T, out_grad)

time: 147 us -> 144 us (0.980)
  waiting for transfers between devices: 22.5 us -> 14.4 us
  blocking collectives: 40.8 us -> 45 us
  starting transfers between devices: 72 us -> 73.5 us
    all_to_all x4, waiting for transfers between devices: 22.5 us -> 14.4 us  [swap(): lax.all_to_all(blocks, axes, split_axis=0, concat_axis=0, tiled=True, axi...]
    all_to_all x1, blocking collectives: 17.5 us -> 21.9 us  [swap(): lax.all_to_all(blocks, axes, split_axis=0, concat_axis=0, tiled=True, axi...]
    all_to_all x4, starting transfers between devices: 72 us -> 73.5 us  [swap(): lax.all_to_all(blocks, axes, split_axis=0, concat_axis=0, tiled=True, axi...]
where the time goes in v5:
time: 144 us
  starting transfers between devices  73.5 us (51%)
  blocking collectives  45 us (31%)
  waiting for transfers between devices  14.4 us (10%)
  Pallas kernels  6.49 us (5%)
  local copies, waits for them, and re-layouts  3.72 us (3%)
    all_to_all x4, starting transfers between devices, swap(): lax.all_to_all(blocks, axes, split_axis=0, concat_axis=0, tiled=True, axi...  73.5 us
    all_to_all x1, blocking collectives, swap(): lax.all_to_all(blocks, axes, split_axis=0, concat_axis=0, tiled=True, axi...  21.9 us
    all_to_all x4, waiting for transfers between devices, swap(): lax.all_to_all(blocks, axes, split_axis=0, concat_axis=0, tiled=True, axi...  14.4 us
    all_gather x1, blocking collectives, shards(): lax.all_gather(layer.transpose(0, 2, 1), 'x', axis=0, tiled=True)  12.5 us
    all_gather x1, blocking collectives, shards(): weights = lax.all_gather(own, 'x', axis=0, tiled=True)  10.5 us
    unnamed x11, local copies, waits for them, and re-layouts  3.59 us
  transfers between devices with their start and end apart: 4, of which 4 were waited for; matrix products, arithmetic and copies ran while one was open for 1% of the time, Pallas kernels for 1%

profile of v5, /device:TPU:1, one launch (start us, length us, event | category | flops | bytes accessed | tf_op | source)
XLA Modules:
  0.0 143.8 jit_solution(10535096898477112630)
XLA Ops:
  0.6 1.8 %copy.15 = bf16[256,8,192]{2,1,0:T(8,128)(2,1)S(1)} copy(bf16[256,8,192]{0,2,1:T(8,128)(2,1)} %param.5) | data formatting | bytes 1572864 | tf_op args[0]
  2.5 0.8 pack_rows.1
  3.2 37.7 %all-to-all-start = ((bf16[32,24,128]{2,1,0:T(8,128)(2,1)}), bf16[32,24,128]{2,1,0:T(8,128)(2,1)S(1)}, u32[]{:S(2)}, u32[]{:S(2)}) async-start(bf16[32,24,128]{2,1,0:T(8,128)(2,1)} %pack_rows.1), calls=%async_computation | async-start | bytes 393216 | tf_op jit(solution)/shard_map/all_to_all | solution.py:307
  41.0 0.5 copy.17.g_ref
  41.5 0.2 copy-done.1
  41.8 10.5 %all_gather.6.w_ref = bf16[256,704]{1,0:T(8,128)(2,1)S(1)} all-gather(bf16[64,704]{1,0:T(8,128)(2,1)S(1)} %pad_maximum_fusion), channel_id=1, replica_groups=mesh['zlo'=8,'zhi'=4,'y'=4,'core'=2,'x'=4] {'x'}, dimensions={0}, use_global_device_ids=true | all-gather | bytes 450560 | tf_op jit(solution)/shard_map/all_gather | solution.py:319
  52.3 0.4 upstream_terms.1
  52.7 2.8 %all-to-all-done.x_ref = bf16[32,24,128]{2,1,0:T(8,128)(2,1)S(1)} async-done(((bf16[32,24,128]{2,1,0:T(8,128)(2,1)}), bf16[32,24,128]{2,1,0:T(8,128)(2,1)S(1)}, u32[]{:S(2)}, u32[]{:S(2)}) %all-to-all-start) | async-done | bytes 196640 | tf_op jit(solution)/shard_map/all_to_all | solution.py:307
  55.4 1.2 layer_terms.1
  56.7 21.9 %all_to_all.25.in_ref = bf16[32,80,128]{2,1,0:T(8,128)(2,1)S(1)} all-to-all(bf16[32,80,128]{2,1,0:T(8,128)(2,1)S(1)} %get-tuple-element.22), channel_id=1, replica_groups=mesh['zlo'=8,'zhi'=4,'y'=4,'core'=2,'x'=4] {'y','core','x'}, dimensions={0} | all-to-all | bytes 1310720 | tf_op jit(solution)/shard_map/all_to_all | solution.py:307
  78.6 0.7 weight_terms.1
  79.3 6.6 %all-to-all-start.2 = ((bf16[8,48,128]{2,1,0:T(8,128)(2,1)}), bf16[8,48,128]{2,1,0:T(8,128)(2,1)S(1)}, u32[]{:S(2)}, u32[]{:S(2)}) async-start(bf16[8,48,128]{2,1,0:T(8,128)(2,1)} %weight_terms.1), calls=%async_computation.2 | async-start | bytes 196608 | tf_op jit(solution)/shard_map/all_to_all | solution.py:307
  86.1 4.8 %all-to-all-done.2.weight_ref = bf16[8,48,128]{2,1,0:T(8,128)(2,1)S(1)} async-done(((bf16[8,48,128]{2,1,0:T(8,128)(2,1)}), bf16[8,48,128]{2,1,0:T(8,128)(2,1)S(1)}, u32[]{:S(2)}, u32[]{:S(2)}) %all-to-all-start.2) | async-done | bytes 98336 | tf_op jit(solution)/shard_map/all_to_all | solution.py:307
  90.9 0.7 replica_terms.1
  91.6 21.5 %all-to-all-start.3 = ((bf16[4,240,128]{2,1,0:T(8,128)(2,1)}), bf16[4,240,128]{2,1,0:T(8,128)(2,1)S(1)}, u32[]{:S(2)}, u32[]{:S(2)}) async-start(bf16[4,240,128]{2,1,0:T(8,128)(2,1)} %replica_terms.1), calls=%async_computation.3 | async-start | bytes 491520 | tf_op jit(solution)/shard_map/all_to_all | solution.py:307
  113.2 12.5 %all_gather.7.in_ref = bf16[8,192,256]{2,1,0:T(8,128)(2,1)S(1)} all-gather(bf16[2,192,256]{2,1,0:T(8,128)(2,1)S(1)} %copy.18), channel_id=1, replica_groups=mesh['zlo'=8,'zhi'=4,'y'=4,'core'=2,'x'=4] {'x'}, dimensions={0}, use_global_device_ids=true | all-gather | bytes 983040 | tf_op jit(solution)/shard_map/all_gather | solution.py:325
  125.7 0.9 settle.1
  126.6 5.4 %all-to-all-done.3.in_ref = bf16[4,240,128]{2,1,0:T(8,128)(2,1)S(1)} async-done(((bf16[4,240,128]{2,1,0:T(8,128)(2,1)}), bf16[4,240,128]{2,1,0:T(8,128)(2,1)S(1)}, u32[]{:S(2)}, u32[]{:S(2)}) %all-to-all-start.3) | async-done | bytes 245792 | tf_op jit(solution)/shard_map/all_to_all | solution.py:307
  132.1 0.6 total_terms.1
  132.7 7.7 %all-to-all-start.4 = ((bf16[8,48,128]{2,1,0:T(8,128)(2,1)}), bf16[8,48,128]{2,1,0:T(8,128)(2,1)S(1)}, u32[]{:S(2)}, u32[]{:S(2)}) async-start(bf16[8,48,128]{2,1,0:T(8,128)(2,1)} %total_terms.1), calls=%async_computation.4 | async-start | bytes 196608 | tf_op jit(solution)/shard_map/all_to_all | solution.py:307
  140.4 0.3 column_terms.1
  140.7 1.0 copy.19
  141.7 1.4 all-to-all-done.4.refs_0_
  143.1 0.7 final_terms.1
  (10 shorter events, 0.3 us)
Async XLA Ops:
  2.5 38.5 %copy-start = (bf16[8,256,192]{1,2,0:T(8,128)(2,1)S(1)}, bf16[8,256,192]{1,2,0:T(8,128)(2,1)}, u32[]{:S(2)}) copy-start(bf16[8,256,192]{1,2,0:T(8,128)(2,1)} %param.9) | copy-start | bytes 2359300
  3.2 52.2 %all-to-all-start = ((bf16[32,24,128]{2,1,0:T(8,128)(2,1)}), bf16[32,24,128]{2,1,0:T(8,128)(2,1)S(1)}, u32[]{:S(2)}, u32[]{:S(2)}) async-start(bf16[32,24,128]{2,1,0:T(8,128)(2,1)} %pack_rows.1), calls=%async_computation | async-start | bytes 393216 | tf_op jit(solution)/shard_map/all_to_all | solution.py:307
  40.9 0.8 copy-start.1
  41.0 0.8 copy-start.2
  41.0 0.8 copy-start.3
  79.3 11.6 %all-to-all-start.2 = ((bf16[8,48,128]{2,1,0:T(8,128)(2,1)}), bf16[8,48,128]{2,1,0:T(8,128)(2,1)S(1)}, u32[]{:S(2)}, u32[]{:S(2)}) async-start(bf16[8,48,128]{2,1,0:T(8,128)(2,1)} %weight_terms.1), calls=%async_computation.2 | async-start | bytes 196608 | tf_op jit(solution)/shard_map/all_to_all | solution.py:307
  91.6 40.5 %all-to-all-start.3 = ((bf16[4,240,128]{2,1,0:T(8,128)(2,1)}), bf16[4,240,128]{2,1,0:T(8,128)(2,1)S(1)}, u32[]{:S(2)}, u32[]{:S(2)}) async-start(bf16[4,240,128]{2,1,0:T(8,128)(2,1)} %replica_terms.1), calls=%async_computation.3 | async-start | bytes 491520 | tf_op jit(solution)/shard_map/all_to_all | solution.py:307
  132.7 10.4 %all-to-all-start.4 = ((bf16[8,48,128]{2,1,0:T(8,128)(2,1)}), bf16[8,48,128]{2,1,0:T(8,128)(2,1)S(1)}, u32[]{:S(2)}, u32[]{:S(2)}) async-start(bf16[8,48,128]{2,1,0:T(8,128)(2,1)} %total_terms.1), calls=%async_computation.4 | async-start | bytes 196608 | tf_op jit(solution)/shard_map/all_to_all | solution.py:307

commit v6 on v5

--- a/solution.py
+++ b/solution.py
@@ -13,6 +13,7 @@
 COLUMN_ORDER = [2, 3, 0, 1]
 FAR_FIRST = [5, 4, 7, 6, 1, 0, 3, 2]
 TABLE_ORDER = [8 * z + c for z in COLUMN_ORDER for c in FAR_FIRST]
+PLANE_ORDER = [4 * c + q for c in FAR_FIRST for q in (2, 3, 0, 1)]
 VMEM_BYTES = 48 * 1024 * 1024
 
 
@@ -143,7 +144,7 @@
             tiles += [lc_sum[rows, :128], lc_sum[rows, 128:]]
             tiles += [proj_sum[rows, :128], proj_sum[rows, 128:]]
             tiles += [out_sum[rows, :128], out_tail[rows]]
-            msg_ref[4 * c + q] = jnp.concatenate(tiles, axis=0).astype(BF)
+            msg_ref[PLANE_ORDER.index(4 * c + q)] = jnp.concatenate(tiles, axis=0).astype(BF)
 
 
 def layer_terms(t, rows, cotangent, weights, ig, igt, base, wt, p):
@@ -194,7 +195,7 @@
 def plane_kernel(in_ref, out_ref):
     wide = []
     for c in range(8):
-        parts = [in_ref[4 * c + q, 0:32].astype(F32)[:, :96] for q in range(4)]
+        parts = [in_ref[PLANE_ORDER.index(4 * c + q), 0:32].astype(F32)[:, :96] for q in range(4)]
         wide.append(jnp.concatenate(parts, axis=1))
     for z in range(4):
         rows = jnp.concatenate([wide[c][8 * z : 8 * z + 8] for c in range(8)], axis=0).astype(BF)
@@ -319,7 +320,7 @@
     weights = lax.all_gather(own, "x", axis=0, tiled=True)
     ig, igt, base, wt, p = upstream_terms(t, cotangent, weights)
     layer, messages = layer_terms(t, rows, cotangent, weights, ig, igt, base, wt, p)
-    received = swap(messages, PLANE)
+    received = swap(messages, PLANE, PLANE_ORDER)
     weight = swap(weight_terms(received, rep_count), "zlo", middle_first)
     column = swap(replica_terms(weight, plane_terms(received)), "zhi", COLUMN_ORDER)
     layer_out = settle(lax.all_gather(layer.transpose(0, 2, 1), "x", axis=0, tiled=True))

time: 144 us -> 143 us (level)
  blocking collectives: 45 us -> 43.3 us
    all_to_all x1, blocking collectives: 21.9 us -> 19.1 us  [swap(): lax.all_to_all(blocks, axes, split_axis=0, concat_axis=0, tiled=True, axi...]
where the time goes in v6:
time: 143 us; the launch traced here: 142 us
  starting transfers between devices  74.7 us (52%)
  blocking collectives  43.3 us (30%)
  waiting for transfers between devices  13.4 us (9%)
  Pallas kernels  6.49 us (5%)
  local copies, waits for them, and re-layouts  3.72 us (3%)
    all_to_all x4, starting transfers between devices, swap(): lax.all_to_all(blocks, axes, split_axis=0, concat_axis=0, tiled=True, axi...  74.7 us
    all_to_all x1, blocking collectives, swap(): lax.all_to_all(blocks, axes, split_axis=0, concat_axis=0, tiled=True, axi...  19.1 us
    all_gather x1, blocking collectives, shards(): lax.all_gather(layer.transpose(0, 2, 1), 'x', axis=0, tiled=True)  13.6 us
    all_to_all x4, waiting for transfers between devices, swap(): lax.all_to_all(blocks, axes, split_axis=0, concat_axis=0, tiled=True, axi...  13.4 us
    all_gather x1, blocking collectives, shards(): weights = lax.all_gather(own, 'x', axis=0, tiled=True)  10.5 us
    unnamed x11, local copies, waits for them, and re-layouts  3.59 us
  transfers between devices with their start and end apart: 4, of which 4 were waited for; matrix products, arithmetic and copies ran while one was open for 1% of the time, Pallas kernels for 1%

profile of v6, /device:TPU:1, one launch (start us, length us, event | category | flops | bytes accessed | tf_op | source)
XLA Modules:
  0.0 142.3 jit_solution(15188711895778612176)
XLA Ops:
  0.6 1.8 %copy.15 = bf16[256,8,192]{2,1,0:T(8,128)(2,1)S(1)} copy(bf16[256,8,192]{0,2,1:T(8,128)(2,1)} %param.5) | data formatting | bytes 1572864 | tf_op args[0]
  2.5 0.8 pack_rows.1
  3.2 37.7 %all-to-all-start = ((bf16[32,24,128]{2,1,0:T(8,128)(2,1)}), bf16[32,24,128]{2,1,0:T(8,128)(2,1)S(1)}, u32[]{:S(2)}, u32[]{:S(2)}) async-start(bf16[32,24,128]{2,1,0:T(8,128)(2,1)} %pack_rows.1), calls=%async_computation | async-start | bytes 393216 | tf_op jit(solution)/shard_map/all_to_all | solution.py:308
  41.0 0.5 copy.17.g_ref
  41.5 0.2 copy-done.1
  41.8 10.5 %all_gather.6.w_ref = bf16[256,704]{1,0:T(8,128)(2,1)S(1)} all-gather(bf16[64,704]{1,0:T(8,128)(2,1)S(1)} %pad_maximum_fusion), channel_id=1, replica_groups=mesh['zlo'=8,'zhi'=4,'y'=4,'core'=2,'x'=4] {'x'}, dimensions={0}, use_global_device_ids=true | all-gather | bytes 450560 | tf_op jit(solution)/shard_map/all_gather | solution.py:320
  52.3 0.4 upstream_terms.1
  52.7 2.8 %all-to-all-done.x_ref = bf16[32,24,128]{2,1,0:T(8,128)(2,1)S(1)} async-done(((bf16[32,24,128]{2,1,0:T(8,128)(2,1)}), bf16[32,24,128]{2,1,0:T(8,128)(2,1)S(1)}, u32[]{:S(2)}, u32[]{:S(2)}) %all-to-all-start) | async-done | bytes 196640 | tf_op jit(solution)/shard_map/all_to_all | solution.py:308
  55.4 1.2 layer_terms.1
  56.7 19.1 %all_to_all.25.in_ref = bf16[32,80,128]{2,1,0:T(8,128)(2,1)S(1)} all-to-all(bf16[32,80,128]{2,1,0:T(8,128)(2,1)S(1)} %get-tuple-element.22), channel_id=1, replica_groups={{22,23,20,21,18,19,16,17,30,31,28,29,26,27,24,25,6,7,4,5,2,3,0,1,14,15,..., dimensions={0} | all-to-all | bytes 1310720 | tf_op jit(solution)/shard_map/all_to_all | solution.py:308
  75.8 0.7 weight_terms.1
  76.5 6.6 %all-to-all-start.2 = ((bf16[8,48,128]{2,1,0:T(8,128)(2,1)}), bf16[8,48,128]{2,1,0:T(8,128)(2,1)S(1)}, u32[]{:S(2)}, u32[]{:S(2)}) async-start(bf16[8,48,128]{2,1,0:T(8,128)(2,1)} %weight_terms.1), calls=%async_computation.2 | async-start | bytes 196608 | tf_op jit(solution)/shard_map/all_to_all | solution.py:308
  83.3 4.8 %all-to-all-done.2.weight_ref = bf16[8,48,128]{2,1,0:T(8,128)(2,1)S(1)} async-done(((bf16[8,48,128]{2,1,0:T(8,128)(2,1)}), bf16[8,48,128]{2,1,0:T(8,128)(2,1)S(1)}, u32[]{:S(2)}, u32[]{:S(2)}) %all-to-all-start.2) | async-done | bytes 98336 | tf_op jit(solution)/shard_map/all_to_all | solution.py:308
  88.1 0.7 replica_terms.1
  88.8 21.8 %all-to-all-start.3 = ((bf16[4,240,128]{2,1,0:T(8,128)(2,1)}), bf16[4,240,128]{2,1,0:T(8,128)(2,1)S(1)}, u32[]{:S(2)}, u32[]{:S(2)}) async-start(bf16[4,240,128]{2,1,0:T(8,128)(2,1)} %replica_terms.1), calls=%async_computation.3 | async-start | bytes 491520 | tf_op jit(solution)/shard_map/all_to_all | solution.py:308
  110.8 13.6 %all_gather.7.in_ref = bf16[8,192,256]{2,1,0:T(8,128)(2,1)S(1)} all-gather(bf16[2,192,256]{2,1,0:T(8,128)(2,1)S(1)} %copy.18), channel_id=1, replica_groups=mesh['zlo'=8,'zhi'=4,'y'=4,'core'=2,'x'=4] {'x'}, dimensions={0}, use_global_device_ids=true | all-gather | bytes 983040 | tf_op jit(solution)/shard_map/all_gather | solution.py:326
  124.4 0.9 settle.1
  125.3 4.2 %all-to-all-done.3.in_ref = bf16[4,240,128]{2,1,0:T(8,128)(2,1)S(1)} async-done(((bf16[4,240,128]{2,1,0:T(8,128)(2,1)}), bf16[4,240,128]{2,1,0:T(8,128)(2,1)S(1)}, u32[]{:S(2)}, u32[]{:S(2)}) %all-to-all-start.3) | async-done | bytes 245792 | tf_op jit(solution)/shard_map/all_to_all | solution.py:308
  129.5 0.6 total_terms.1
  130.2 8.5 %all-to-all-start.4 = ((bf16[8,48,128]{2,1,0:T(8,128)(2,1)}), bf16[8,48,128]{2,1,0:T(8,128)(2,1)S(1)}, u32[]{:S(2)}, u32[]{:S(2)}) async-start(bf16[8,48,128]{2,1,0:T(8,128)(2,1)} %total_terms.1), calls=%async_computation.4 | async-start | bytes 196608 | tf_op jit(solution)/shard_map/all_to_all | solution.py:308
  138.7 0.3 column_terms.1
  139.0 1.0 copy.19
  140.0 1.7 %all-to-all-done.4.refs_0_ = bf16[8,48,128]{2,1,0:T(8,128)(2,1)S(1)} async-done(((bf16[8,48,128]{2,1,0:T(8,128)(2,1)}), bf16[8,48,128]{2,1,0:T(8,128)(2,1)S(1)}, u32[]{:S(2)}, u32[]{:S(2)}) %all-to-all-start.4) | async-done | bytes 98336 | tf_op jit(solution)/shard_map/all_to_all | solution.py:308
  141.6 0.7 final_terms.1
  (10 shorter events, 0.3 us)
Async XLA Ops:
  2.5 38.5 %copy-start = (bf16[8,256,192]{1,2,0:T(8,128)(2,1)S(1)}, bf16[8,256,192]{1,2,0:T(8,128)(2,1)}, u32[]{:S(2)}) copy-start(bf16[8,256,192]{1,2,0:T(8,128)(2,1)} %param.9) | copy-start | bytes 2359300
  3.2 52.2 %all-to-all-start = ((bf16[32,24,128]{2,1,0:T(8,128)(2,1)}), bf16[32,24,128]{2,1,0:T(8,128)(2,1)S(1)}, u32[]{:S(2)}, u32[]{:S(2)}) async-start(bf16[32,24,128]{2,1,0:T(8,128)(2,1)} %pack_rows.1), calls=%async_computation | async-start | bytes 393216 | tf_op jit(solution)/shard_map/all_to_all | solution.py:308
  40.9 0.8 copy-start.1
  41.0 0.8 copy-start.2
  41.0 0.8 copy-start.3
  76.5 11.6 %all-to-all-start.2 = ((bf16[8,48,128]{2,1,0:T(8,128)(2,1)}), bf16[8,48,128]{2,1,0:T(8,128)(2,1)S(1)}, u32[]{:S(2)}, u32[]{:S(2)}) async-start(bf16[8,48,128]{2,1,0:T(8,128)(2,1)} %weight_terms.1), calls=%async_computation.2 | async-start | bytes 196608 | tf_op jit(solution)/shard_map/all_to_all | solution.py:308
  88.8 40.7 %all-to-all-start.3 = ((bf16[4,240,128]{2,1,0:T(8,128)(2,1)}), bf16[4,240,128]{2,1,0:T(8,128)(2,1)S(1)}, u32[]{:S(2)}, u32[]{:S(2)}) async-start(bf16[4,240,128]{2,1,0:T(8,128)(2,1)} %replica_terms.1), calls=%async_computation.3 | async-start | bytes 491520 | tf_op jit(solution)/shard_map/all_to_all | solution.py:308
  130.2 11.5 %all-to-all-start.4 = ((bf16[8,48,128]{2,1,0:T(8,128)(2,1)}), bf16[8,48,128]{2,1,0:T(8,128)(2,1)S(1)}, u32[]{:S(2)}, u32[]{:S(2)}) async-start(bf16[8,48,128]{2,1,0:T(8,128)(2,1)} %total_terms.1), calls=%async_computation.4 | async-start | bytes 196608 | tf_op jit(solution)/shard_map/all_to_all | solution.py:308

commit v7 on v6

--- a/solution.py
+++ b/solution.py
@@ -34,30 +34,36 @@
     return pl.BlockSpec(shape, lambda i, t: zeros)
 
 
-def pack_kernel(t_ref, pooled_ref, out_ref):
-    first = pooled_ref[:, 0, 0].astype(F32)
-    second = pooled_ref[:, 0, 1].astype(F32)
-    mixed = jnp.concatenate([first[:, :, 128:], second[:, :, 128:]], axis=2)
-    rows = jnp.concatenate([first[:, :, :128], second[:, :, :128], mixed], axis=1)
-    rows = rows.astype(BF)
+def pack_kernel(t_ref, pooled_ref, out_ref, plane_ref):
+    row = lax.broadcasted_iota(jnp.int32, (64, 256), 0)
+    lane = lax.broadcasted_iota(jnp.int32, (64, 256), 1)
+    wanted = 8 * (row % 32) + 2 * t_ref[0] + row // 32
+    chosen = jnp.where(lane == wanted, 1.0, 0.0).astype(BF)
+    for e in range(8):
+        picked = dot_t(chosen, pooled_ref[e])
+        first, second = picked[:32], picked[32:]
+        plane_ref[0, pl.ds(e, 32, stride=8), :] = first[:, :128]
+        plane_ref[1, pl.ds(e, 32, stride=8), :] = second[:, :128]
+        plane_ref[2, pl.ds(e, 32, stride=8), :] = jnp.concatenate([first[:, 128:], second[:, 128:]], axis=1)
+    rows = jnp.concatenate([plane_ref[i].reshape(32, 8, 128) for i in range(3)], axis=1).astype(BF)
     for k, d in enumerate(TABLE_ORDER):
         out_ref[k] = rows[d]
 
 
 def pack_rows(t, pooled):
-    view = pooled.reshape(32, 4, 2, 8, 192)
     return pl.pallas_call(
         pack_kernel,
         grid_spec=pltpu.PrefetchScalarGridSpec(
             num_scalar_prefetch=1,
             grid=(1,),
-            in_specs=[pl.BlockSpec((32, 1, 2, 8, 192), lambda i, t: (0, t[0], 0, 0, 0))],
+            in_specs=[whole((8, 192, 256))],
             out_specs=whole((32, 24, 128)),
+            scratch_shapes=[pltpu.VMEM((3, 256, 128), F32)],
         ),
         out_shape=jax.ShapeDtypeStruct((32, 24, 128), BF),
         compiler_params=params(),
         name="pack_rows",
-    )(t, view)
+    )(t, pooled.transpose(1, 2, 0))
 
 
 def upstream_kernel(t_ref, g_ref, w_ref, ig_ref, igt_ref, base_ref, wt_ref, p_ref):

time: 143 us -> 143 us (level)
    unnamed x11 -> x12, local copies, waits for them, and re-layouts: 3.59 us -> 2.9 us
where the time goes in v7:
time: 143 us; the launch traced here: 142 us
  starting transfers between devices  74.7 us (52%)
  blocking collectives  43.3 us (30%)
  waiting for transfers between devices  13.4 us (9%)
  Pallas kernels  6.87 us (5%)
  local copies, waits for them, and re-layouts  3.03 us (2%)
    all_to_all x4, starting transfers between devices, swap(): lax.all_to_all(blocks, axes, split_axis=0, concat_axis=0, tiled=True, axi...  74.7 us
    all_to_all x1, blocking collectives, swap(): lax.all_to_all(blocks, axes, split_axis=0, concat_axis=0, tiled=True, axi...  19.1 us
    all_gather x1, blocking collectives, shards(): lax.all_gather(layer.transpose(0, 2, 1), 'x', axis=0, tiled=True)  13.6 us
    all_to_all x4, waiting for transfers between devices, swap(): lax.all_to_all(blocks, axes, split_axis=0, concat_axis=0, tiled=True, axi...  13.4 us
    all_gather x1, blocking collectives, shards(): weights = lax.all_gather(own, 'x', axis=0, tiled=True)  10.5 us
    unnamed x12, local copies, waits for them, and re-layouts  2.9 us
  transfers between devices with their start and end apart: 4, of which 4 were waited for; matrix products, arithmetic and copies ran while one was open for 1% of the time, Pallas kernels for 1%

profile of v7, /device:TPU:1, one launch (start us, length us, event | category | flops | bytes accessed | tf_op | source)
XLA Modules:
  0.0 142.0 jit_solution(2405972831613014178)
XLA Ops:
  0.6 1.1 copy-done
  1.8 1.1 pack_rows.1
  2.9 37.7 %all-to-all-start = ((bf16[32,24,128]{2,1,0:T(8,128)(2,1)}), bf16[32,24,128]{2,1,0:T(8,128)(2,1)S(1)}, u32[]{:S(2)}, u32[]{:S(2)}) async-start(bf16[32,24,128]{2,1,0:T(8,128)(2,1)} %pack_rows.1), calls=%async_computation | async-start | bytes 393216 | tf_op jit(solution)/shard_map/all_to_all | solution.py:314
  40.6 0.5 copy.15.g_ref
  41.2 0.2 copy-done.2
  41.4 10.5 %all_gather.6.w_ref = bf16[256,704]{1,0:T(8,128)(2,1)S(1)} all-gather(bf16[64,704]{1,0:T(8,128)(2,1)S(1)} %pad_maximum_fusion), channel_id=1, replica_groups=mesh['zlo'=8,'zhi'=4,'y'=4,'core'=2,'x'=4] {'x'}, dimensions={0}, use_global_device_ids=true | all-gather | bytes 450560 | tf_op jit(solution)/shard_map/all_gather | solution.py:326
  51.9 0.4 upstream_terms.1
  52.4 2.8 %all-to-all-done.x_ref = bf16[32,24,128]{2,1,0:T(8,128)(2,1)S(1)} async-done(((bf16[32,24,128]{2,1,0:T(8,128)(2,1)}), bf16[32,24,128]{2,1,0:T(8,128)(2,1)S(1)}, u32[]{:S(2)}, u32[]{:S(2)}) %all-to-all-start) | async-done | bytes 196640 | tf_op jit(solution)/shard_map/all_to_all | solution.py:314
  55.1 1.2 layer_terms.1
  56.3 19.1 %all_to_all.25.in_ref = bf16[32,80,128]{2,1,0:T(8,128)(2,1)S(1)} all-to-all(bf16[32,80,128]{2,1,0:T(8,128)(2,1)S(1)} %get-tuple-element.22), channel_id=1, replica_groups={{22,23,20,21,18,19,16,17,30,31,28,29,26,27,24,25,6,7,4,5,2,3,0,1,14,15,..., dimensions={0} | all-to-all | bytes 1310720 | tf_op jit(solution)/shard_map/all_to_all | solution.py:314
  75.5 0.7 weight_terms.1
  76.2 6.6 %all-to-all-start.2 = ((bf16[8,48,128]{2,1,0:T(8,128)(2,1)}), bf16[8,48,128]{2,1,0:T(8,128)(2,1)S(1)}, u32[]{:S(2)}, u32[]{:S(2)}) async-start(bf16[8,48,128]{2,1,0:T(8,128)(2,1)} %weight_terms.1), calls=%async_computation.2 | async-start | bytes 196608 | tf_op jit(solution)/shard_map/all_to_all | solution.py:314
  83.0 4.8 %all-to-all-done.2.weight_ref = bf16[8,48,128]{2,1,0:T(8,128)(2,1)S(1)} async-done(((bf16[8,48,128]{2,1,0:T(8,128)(2,1)}), bf16[8,48,128]{2,1,0:T(8,128)(2,1)S(1)}, u32[]{:S(2)}, u32[]{:S(2)}) %all-to-all-start.2) | async-done | bytes 98336 | tf_op jit(solution)/shard_map/all_to_all | solution.py:314
  87.8 0.7 replica_terms.1
  88.5 21.8 %all-to-all-start.3 = ((bf16[4,240,128]{2,1,0:T(8,128)(2,1)}), bf16[4,240,128]{2,1,0:T(8,128)(2,1)S(1)}, u32[]{:S(2)}, u32[]{:S(2)}) async-start(bf16[4,240,128]{2,1,0:T(8,128)(2,1)} %replica_terms.1), calls=%async_computation.3 | async-start | bytes 491520 | tf_op jit(solution)/shard_map/all_to_all | solution.py:314
  110.4 13.6 %all_gather.7.in_ref = bf16[8,192,256]{2,1,0:T(8,128)(2,1)S(1)} all-gather(bf16[2,192,256]{2,1,0:T(8,128)(2,1)S(1)} %copy.16), channel_id=1, replica_groups=mesh['zlo'=8,'zhi'=4,'y'=4,'core'=2,'x'=4] {'x'}, dimensions={0}, use_global_device_ids=true | all-gather | bytes 983040 | tf_op jit(solution)/shard_map/all_gather | solution.py:332
  124.1 0.9 settle.1
  125.0 4.2 %all-to-all-done.3.in_ref = bf16[4,240,128]{2,1,0:T(8,128)(2,1)S(1)} async-done(((bf16[4,240,128]{2,1,0:T(8,128)(2,1)}), bf16[4,240,128]{2,1,0:T(8,128)(2,1)S(1)}, u32[]{:S(2)}, u32[]{:S(2)}) %all-to-all-start.3) | async-done | bytes 245792 | tf_op jit(solution)/shard_map/all_to_all | solution.py:314
  129.2 0.7 total_terms.1
  129.9 8.5 %all-to-all-start.4 = ((bf16[8,48,128]{2,1,0:T(8,128)(2,1)}), bf16[8,48,128]{2,1,0:T(8,128)(2,1)S(1)}, u32[]{:S(2)}, u32[]{:S(2)}) async-start(bf16[8,48,128]{2,1,0:T(8,128)(2,1)} %total_terms.1), calls=%async_computation.4 | async-start | bytes 196608 | tf_op jit(solution)/shard_map/all_to_all | solution.py:314
  138.4 0.3 column_terms.1
  138.7 1.0 copy.17
  139.7 1.7 %all-to-all-done.4.refs_0_ = bf16[8,48,128]{2,1,0:T(8,128)(2,1)S(1)} async-done(((bf16[8,48,128]{2,1,0:T(8,128)(2,1)}), bf16[8,48,128]{2,1,0:T(8,128)(2,1)S(1)}, u32[]{:S(2)}, u32[]{:S(2)}) %all-to-all-start.4) | async-done | bytes 98336 | tf_op jit(solution)/shard_map/all_to_all | solution.py:314
  141.3 0.7 final_terms.1
  (11 shorter events, 0.3 us)
Async XLA Ops:
  0.6 1.1 copy-start
  1.8 38.8 %copy-start.1 = (bf16[8,256,192]{1,2,0:T(8,128)(2,1)S(1)}, bf16[8,256,192]{1,2,0:T(8,128)(2,1)}, u32[]{:S(2)}) copy-start(bf16[8,256,192]{1,2,0:T(8,128)(2,1)} %param.9) | copy-start | bytes 2359300
  2.9 52.2 %all-to-all-start = ((bf16[32,24,128]{2,1,0:T(8,128)(2,1)}), bf16[32,24,128]{2,1,0:T(8,128)(2,1)S(1)}, u32[]{:S(2)}, u32[]{:S(2)}) async-start(bf16[32,24,128]{2,1,0:T(8,128)(2,1)} %pack_rows.1), calls=%async_computation | async-start | bytes 393216 | tf_op jit(solution)/shard_map/all_to_all | solution.py:314
  40.6 0.8 copy-start.2
  40.6 0.8 copy-start.3
  40.6 0.8 copy-start.4
  76.2 11.6 %all-to-all-start.2 = ((bf16[8,48,128]{2,1,0:T(8,128)(2,1)}), bf16[8,48,128]{2,1,0:T(8,128)(2,1)S(1)}, u32[]{:S(2)}, u32[]{:S(2)}) async-start(bf16[8,48,128]{2,1,0:T(8,128)(2,1)} %weight_terms.1), calls=%async_computation.2 | async-start | bytes 196608 | tf_op jit(solution)/shard_map/all_to_all | solution.py:314
  88.5 40.7 %all-to-all-start.3 = ((bf16[4,240,128]{2,1,0:T(8,128)(2,1)}), bf16[4,240,128]{2,1,0:T(8,128)(2,1)S(1)}, u32[]{:S(2)}, u32[]{:S(2)}) async-start(bf16[4,240,128]{2,1,0:T(8,128)(2,1)} %replica_terms.1), calls=%async_computation.3 | async-start | bytes 491520 | tf_op jit(solution)/shard_map/all_to_all | solution.py:314
  129.9 11.5 %all-to-all-start.4 = ((bf16[8,48,128]{2,1,0:T(8,128)(2,1)}), bf16[8,48,128]{2,1,0:T(8,128)(2,1)S(1)}, u32[]{:S(2)}, u32[]{:S(2)}) async-start(bf16[8,48,128]{2,1,0:T(8,128)(2,1)} %total_terms.1), calls=%async_computation.4 | async-start | bytes 196608 | tf_op jit(solution)/shard_map/all_to_all | solution.py:314
